TPU v7x, 32 devices: a whole 2x2x4 slice. The times are simulated.
32 devices in a mesh: dp: 8 (over z, x), tensor: 4 (over y, core).
Axes of the slice: x: 2, y: 2, z: 4, core: 2. Of those that a mesh axis runs over, the one named last changes fastest.
Arguments:
- hidden: bfloat16 [2048, 8192], P(('dp', 'tensor')), may hold values from -6 to 6
- cotangent: bfloat16 [2048, 2048], P('dp', 'tensor'), may hold values from -6 to 6
- frozen_key_value: bfloat16 [8192, 2048], P(None, 'tensor'), may hold values from -0.0625 to 0.0625
- adapter_down_factors: bfloat16 [8192, 512], P('tensor'), may hold values from -0.0625 to 0.0625
- adapter_up_factors: bfloat16 [512, 2048], P(None, 'tensor'), may hold values from -0.75 to 0.75
- down_master_copy: float32 [8192, 512], P('tensor', 'dp'), may hold values from -0.0625 to 0.0625
- down_first_moment: float32 [8192, 512], P('tensor', 'dp'), may hold values from -1.5 to 1.5
- down_second_moment: float32 [8192, 512], P('tensor', 'dp'), may hold values from 0.001 to 0.05
- up_master_copy: float32 [512, 2048], P('dp', 'tensor'), may hold values from -0.75 to 0.75
- up_first_moment: float32 [512, 2048], P('dp', 'tensor'), may hold values from -0.3125 to 0.3125
- up_second_moment: float32 [512, 2048], P('dp', 'tensor'), may hold values from 1e-05 to 0.001
- adapter_of_token: int32 [2048, 1], P('dp'), may hold values from 0 to 7; in each aligned block of 256 rows (0 to 255, 256 to 511, ...) at most 64 rows name the same one
- adapter_rank_bucket: int32 [8], replicated, may hold values from 0 to 3
- adapter_owner_slot: int32 [8], replicated, may hold values from 0 to 7, each once
- live_token_counts: int32 [8], replicated, may hold values from 64 to 256, as said below
Outputs:
- hidden_gradient: bfloat16 [2048, 8192], P(('dp', 'tensor'))
- new_down_master: float32 [8192, 512], P('tensor', 'dp')
- new_down_moment: float32 [8192, 512], P('tensor', 'dp')
- new_down_second: float32 [8192, 512], P('tensor', 'dp')
- new_up_master: float32 [512, 2048], P('dp', 'tensor')
- new_up_moment: float32 [512, 2048], P('dp', 'tensor')
- new_up_second: float32 [512, 2048], P('dp', 'tensor')
Inputs may be any that keep to these rules, and one draw needn't show every extreme that they name: `adapter_of_token`: in the rows of one index of dp (aligned blocks of 256 rows) no adapter is named by more than 64 rows, and some adapter reaches 64; every adapter is named somewhere. `adapter_owner_slot`: each slot once. `live_token_counts`: some shard is full.
All inputs are finite; a program needn't handle non-finite values.
Results may differ from a plain program's by a relative error of at most 0.0034.
Values may be sent and summed in bfloat16 or wider, within the bound.
A program may use at most 128 MiB of HBM per device.

v0:
```python
import jax
import jax.numpy as jnp
from jax import lax
from jax.sharding import PartitionSpec as P

RMIN = 8
PADDED_RANK = 64


adapter_alpha_scale = 16.0
beta_one = 0.9
beta_two = 0.999
adam_eps = 1e-08
learn_rate = 0.0002
weight_decay = 0.1
first_fix = 0.9999734386011124
second_fix = 0.09520785288629038


def adapter_tables(adapter_of_token, adapter_rank_bucket, adapter_owner_slot):
    adapter = adapter_of_token[:, 0]
    idents = jnp.arange(adapter_owner_slot.shape[0], dtype=jnp.int32)
    slot_hit = (adapter[:, None] == idents[None, :]).astype(jnp.int32)
    slot_of = jnp.sum(slot_hit * adapter_owner_slot[None, :], axis=1)
    bucket = jnp.sum(slot_hit * adapter_rank_bucket[None, :], axis=1)
    steps_up = (
        1
        + (bucket >= 1).astype(jnp.int32)
        + 2 * (bucket >= 2).astype(jnp.int32)
        + 4 * (bucket >= 3).astype(jnp.int32)
    )
    return (slot_of, RMIN * steps_up)


def adamw(master, moment, second, grad):
    new_moment = beta_one * moment + (1.0 - beta_one) * grad
    new_second = beta_two * second + (1.0 - beta_two) * grad * grad
    update = new_moment / first_fix / (jnp.sqrt(new_second / second_fix) + adam_eps)
    new_master = master - learn_rate * (update + weight_decay * master)
    return (new_master, new_moment, new_second)


def contract_helper(left, right, left_dim, right_dim):
    return lax.dot_general(
        left, right, (((left_dim,), (right_dim,)), ((), ())), preferred_element_type=jnp.float32
    )


def local(
    hidden,
    cotangent,
    frozen_key_value,
    adapter_down_factors,
    adapter_up_factors,
    down_master_copy,
    down_first_moment,
    down_second_moment,
    up_master_copy,
    up_first_moment,
    up_second_moment,
    adapter_of_token,
    adapter_rank_bucket,
    adapter_owner_slot,
    live_token_counts,
):
    n_tensor = lax.axis_size("tensor")
    token_row_block = cotangent.shape[0]
    width = hidden.shape[1]
    shard_columns = width // n_tensor
    slot_count_total = adapter_owner_slot.shape[0]
    tensor_position = lax.axis_index("tensor")
    gathered = lax.all_gather(hidden, "tensor", axis=0, tiled=True)
    hidden_columns = lax.dynamic_slice_in_dim(
        gathered, tensor_position * shard_columns, shard_columns, 1
    )
    row_limit = lax.dynamic_index_in_dim(live_token_counts, lax.axis_index("dp"), 0, keepdims=False)
    is_valid = jnp.arange(token_row_block, dtype=jnp.int32) < row_limit
    masked_cotangent = jnp.where(is_valid[:, None], cotangent, jnp.zeros_like(cotangent))
    slot_of, rank_lookup = adapter_tables(adapter_of_token, adapter_rank_bucket, adapter_owner_slot)
    idents = jnp.arange(slot_count_total, dtype=jnp.int32)
    slot_hit = (slot_of[:, None] == idents[None, :]).astype(jnp.float32)
    down_partial = jnp.dot(
        hidden_columns, adapter_down_factors, preferred_element_type=jnp.float32
    ).reshape(token_row_block, slot_count_total, PADDED_RANK)
    up_partial = contract_helper(masked_cotangent, adapter_up_factors, 1, 1).reshape(
        token_row_block, slot_count_total, PADDED_RANK
    )
    down_own = jnp.einsum("tsk,ts->tk", down_partial, slot_hit)
    up_own = jnp.einsum("tsk,ts->tk", up_partial, slot_hit)
    down_sum, up_sum = lax.psum((down_own, up_own), "tensor")
    kept_cols = jnp.arange(PADDED_RANK, dtype=jnp.int32)[None, :] < rank_lookup[:, None]
    alpha_rank_ratio = (adapter_alpha_scale / rank_lookup.astype(jnp.float32))[:, None]
    factor = jnp.where(kept_cols, alpha_rank_ratio, jnp.zeros_like(alpha_rank_ratio))
    down_weight = (down_sum * factor).astype(jnp.bfloat16)
    up_weight = (up_sum * factor).astype(jnp.bfloat16)
    hit_half = slot_hit.astype(jnp.bfloat16)
    positioned_up_factors = (up_weight[:, None, :] * hit_half[:, :, None]).reshape(
        token_row_block, slot_count_total * PADDED_RANK
    )
    adapter_extra_output = contract_helper(positioned_up_factors, adapter_down_factors, 1, 1)
    frozen_input_term = contract_helper(masked_cotangent, frozen_key_value, 1, 1)
    current_block = lax.dynamic_slice_in_dim(
        frozen_input_term, tensor_position * shard_columns, shard_columns, 1
    )
    frozen_input_term = lax.dynamic_update_slice_in_dim(
        frozen_input_term, current_block + adapter_extra_output, tensor_position * shard_columns, 1
    )
    reduced = lax.psum_scatter(frozen_input_term, "tensor", scatter_dimension=0, tiled=True)
    hidden_gradient = reduced.astype(jnp.bfloat16)
    placed_down = (down_weight[:, None, :] * hit_half[:, :, None]).reshape(
        token_row_block, slot_count_total * PADDED_RANK
    )
    grad_all_down = contract_helper(hidden_columns, positioned_up_factors, 0, 0)
    grad_all_up = contract_helper(placed_down, masked_cotangent, 0, 0)
    grad_down, grad_up = (
        lax.psum_scatter(grad_all_down, "dp", scatter_dimension=1, tiled=True),
        lax.psum_scatter(grad_all_up, "dp", scatter_dimension=0, tiled=True),
    )
    grad_down = grad_down / token_row_block
    grad_up = grad_up / token_row_block
    new_dm, new_dmo, new_ds = adamw(
        down_master_copy, down_first_moment, down_second_moment, grad_down
    )
    new_um, new_umo, new_us = adamw(up_master_copy, up_first_moment, up_second_moment, grad_up)
    return (hidden_gradient, new_dm, new_dmo, new_ds, new_um, new_umo, new_us)


def solution(mesh):
    return jax.shard_map(
        local,
        mesh=mesh,
        in_specs=(
            P(("dp", "tensor"), None),
            P("dp", "tensor"),
            P(None, "tensor"),
            P("tensor", None),
            P(None, "tensor"),
            P("tensor", "dp"),
            P("tensor", "dp"),
            P("tensor", "dp"),
            P("dp", "tensor"),
            P("dp", "tensor"),
            P("dp", "tensor"),
            P("dp", None),
            P(),
            P(),
            P(),
        ),
        out_specs=(
            P(("dp", "tensor"), None),
            P("tensor", "dp"),
            P("tensor", "dp"),
            P("tensor", "dp"),
            P("dp", "tensor"),
            P("dp", "tensor"),
            P("dp", "tensor"),
        ),
        check_vma=False,
    )
```

profile of v0, /device:TPU:0, one launch (start us, length us, event | category | flops | bytes accessed | tf_op | source)
XLA Modules:
  0.0 323.1 jit_solution(10206056091784818499)
XLA Ops:
  7.2 0.0 copy-start
  7.2 0.0 copy-start.1
  7.2 0.0 all-gather.2.cloned.1.call-start
  7.2 0.7 all-gather.2.cloned.1.call-update
  7.9 0.0 all-reduce.3.cloned.1.call-start
  8.0 1.2 dynamic_slice.10
  9.2 0.6 iota_compare_fusion.3
  9.9 0.8 select_reduce_fusion
  10.7 1.5 fusion.16
  12.2 34.6 %all-gather.2.cloned.1.call-done = bf16[256,8192]{1,0:T(8,128)(2,1)} async-done(((bf16[64,8192]{1,0:T(8,128)(2,1)}), bf16[256,8192]{1,0:T(8,128)(2,1)}) %all-gather.2.cloned.1.call-update) | async-done | bytes 4194320 | tf_op jit(solution)/shard_map/all_gather | solution.py:72
  46.8 2.1 fusion.1
  49.0 0.8 multiply_reduce_fusion
  49.7 0.0 all-reduce.3.cloned.1.call-update
  49.7 0.0 reduce-scatter.8.cloned.1.call-start
  49.8 31.6 %all-reduce.3.cloned.1.call-done = (f32[256,64]{0,1:T(8,128)}, f32[256,64]{0,1:T(8,128)}) async-done(((f32[256,64]{0,1:T(8,128)}, f32[256,64]{0,1:T(8,128)}), (f32[256,64]{0,1:T(8,128)}, f32[256,64]{0,1:T(8,128)})) %all-reduce.3.cloned.1.call-update) | async-done | bytes 131088 | tf_op jit(solution)/shard_map/psum | solution.py:90
  81.4 0.9 fusion.6
  82.4 1.3 fusion.15
  83.7 0.0 reduce-scatter.8.cloned.1.call-update
  83.7 0.0 reduce-scatter.6.cloned.1.call-start
  83.8 3.9 %fusion.3 = f32[2048,512]{0,1:T(8,128)} fusion(bf16[256,512]{0,1:T(8,128)(2,1)S(1)} %bitcast.13, bf16[256,8192]{1,0:T(8,128)(2,1)} %all-gather.2.cloned.1.call-done, s32[]{:T(128)S(6)} %select_n.19), kind=kOutput, calls=%fused_computation.4 | convolution fusion | flops 536870912 | bytes 5505028 | tf_op jit(solution)/shard_map/dot_general | solution.py:44
  87.7 0.0 reduce-scatter.6.cloned.1.call-update
  87.7 0.0 reduce-scatter.4.cloned.1.call-start
  87.8 9.0 %fusion.17 = f32[256,8192]{1,0:T(8,128)} fusion(bf16[8192,512]{1,0:T(8,128)(2,1)} %param.17, bf16[256,512]{1,0:T(8,128)(2,1)S(1)} %copy-done.1, pred[256]{0:T(512)(128)(4,1)S(1)} %iota_compare_fusion.3), kind=kOutput, calls=%fused_computation.41 | convolution fusion | flops 2147614720 | bytes 17039616 | tf_op jit(solution)/shard_map/dot_general | solution.py:44
  96.8 3.7 %fusion = f32[256,8192]{1,0:T(8,128)} fusion(f32[256,8192]{1,0:T(8,128)} %fusion.17, s32[]{:T(128)S(6)} %select_n.19, bf16[256,512]{0,1:T(8,128)(2,1)S(1)} %bitcast.14, bf16[2048,512]{1,0:T(8,128)(2,1)S(1)} %copy-done), kind=kOutput, calls=%fused_computation.1 | convolution fusion | flops 537395200 | bytes 6553604 | tf_op jit(solution)/shard_map/dot_general | solution.py:44
  100.5 0.0 copy-start.3
  100.5 0.0 reduce-scatter.4.cloned.1.call-update
  100.5 48.8 %reduce-scatter.8.cloned.1.call-done = f32[64,512]{1,0:T(8,128)} async-done(((f32[512,512]{1,0:T(8,128)}), f32[64,512]{1,0:T(8,128)}) %reduce-scatter.8.cloned.1.call-update) | async-done | bytes 131088 | tf_op jit(solution)/shard_map/reduce_scatter | solution.py:117
  149.3 1.7 multiply_subtract_fusion.1
  151.1 88.7 %reduce-scatter.6.cloned.1.call-done = f32[2048,64]{0,1:T(8,128)} async-done(((f32[2048,512]{0,1:T(8,128)}), f32[2048,64]{0,1:T(8,128)}) %reduce-scatter.6.cloned.1.call-update) | async-done | bytes 524304 | tf_op jit(solution)/shard_map/reduce_scatter | solution.py:116
  239.8 2.6 multiply_subtract_fusion
  242.3 71.5 %reduce-scatter.4.cloned.1.call-done = f32[64,8192]{1,0:T(8,128)} async-done(((f32[256,8192]{1,0:T(8,128)}), f32[64,8192]{1,0:T(8,128)}) %reduce-scatter.4.cloned.1.call-update) | async-done | bytes 2097168 | tf_op jit(solution)/shard_map/reduce_scatter | solution.py:108
  313.9 2.7 convert_element_type.48
  (14 shorter events, 0.1 us)
Async XLA Ops:
  7.2 39.6 %copy-start = (bf16[2048,512]{1,0:T(8,128)(2,1)S(1)}, bf16[2048,512]{1,0:T(8,128)(2,1)}, u32[]{:S(2)}) copy-start(bf16[2048,512]{1,0:T(8,128)(2,1)} %param.18) | copy-start | bytes 6291460
  7.2 75.2 %copy-start.1 = (bf16[256,512]{1,0:T(8,128)(2,1)S(1)}, bf16[256,512]{1,0:T(8,128)(2,1)}, u32[]{:S(2)}) copy-start(bf16[256,512]{1,0:T(8,128)(2,1)} %param.16) | copy-start | bytes 786436
  7.2 39.6 %all-gather.2.cloned.1.call-start = ((), (), s32[]{:S(2)}) async-start(), calls=%async_computation.4 | async-start | bytes 5242880 | tf_op jit(solution)/shard_map/all_gather | solution.py:72
  7.9 73.5 %all-reduce.3.cloned.1.call-start = ((), (), s32[]{:S(2)}) async-start(), calls=%async_computation.7 | async-start | bytes 262144 | tf_op jit(solution)/shard_map/psum | solution.py:90
  49.7 99.6 %reduce-scatter.8.cloned.1.call-start = ((), (), s32[]{:S(2)}) async-start(), calls=%async_computation.6 | async-start | bytes 1179648 | tf_op jit(solution)/shard_map/reduce_scatter | solution.py:117
  83.7 156.0 %reduce-scatter.6.cloned.1.call-start = ((), (), s32[]{:S(2)}) async-start(), calls=%async_computation.5 | async-start | bytes 4718592 | tf_op jit(solution)/shard_map/reduce_scatter | solution.py:116
  87.7 226.1 %reduce-scatter.4.cloned.1.call-start = ((), (), s32[]{:S(2)}) async-start(), calls=%async_computation.3 | async-start | bytes 10485760 | tf_op jit(solution)/shard_map/reduce_scatter | solution.py:108
  100.5 48.9 %copy-start.4 = (f32[64,512]{1,0:T(8,128)S(1)}, f32[64,512]{1,0:T(8,128)}, u32[]{:S(2)}) copy-start(f32[64,512]{1,0:T(8,128)} %param.23) | copy-start | bytes 393220
  100.5 48.9 %copy-start.5 = (f32[64,512]{1,0:T(8,128)S(1)}, f32[64,512]{1,0:T(8,128)}, u32[]{:S(2)}) copy-start(f32[64,512]{1,0:T(8,128)} %param.24) | copy-start | bytes 393220
  100.5 48.9 %copy-start.6 = (f32[64,512]{1,0:T(8,128)S(1)}, f32[64,512]{1,0:T(8,128)}, u32[]{:S(2)}) copy-start(f32[64,512]{1,0:T(8,128)} %param.25) | copy-start | bytes 393220
  100.5 139.3 %copy-start.2 = (f32[2048,64]{0,1:T(8,128)S(1)}, f32[2048,64]{0,1:T(8,128)}, u32[]{:S(2)}) copy-start(f32[2048,64]{0,1:T(8,128)} %param.20) | copy-start | bytes 1572868
  100.5 139.3 %copy-start.3 = (f32[2048,64]{0,1:T(8,128)S(1)}, f32[2048,64]{0,1:T(8,128)}, u32[]{:S(2)}) copy-start(f32[2048,64]{0,1:T(8,128)} %param.21) | copy-start | bytes 1572868
Sparse Core Ops, SparseCore 0:
  9.6 37.1 all-gather.1
  49.9 31.5 all-reduce.2
  85.8 63.4 reduce-scatter.7
  152.8 86.8 reduce-scatter.5
  242.3 71.4 reduce-scatter.3
where the time goes:
time: 324 us; the launch traced here: 323 us
  waiting for transfers between devices  276 us (85%)
  matrix products  21.6 us (7%)
  between operations  13.9 us (4%)
  other arithmetic  10.1 us (3%)
    reduce_scatter x1, waiting for transfers between devices, local(): lax.psum_scatter(grad_all_down, 'dp', scatter_dimension=1, tiled=True)  88.7 us
    reduce_scatter x1, waiting for transfers between devices, local(): lax.psum_scatter(frozen_input_term, 'tensor', scatter_dimension=0, tiled=...  71.5 us
    reduce_scatter x1, waiting for transfers between devices, local(): lax.psum_scatter(grad_all_up, 'dp', scatter_dimension=0, tiled=True)  48.8 us
    all_gather x1, waiting for transfers between devices, local(): gathered = lax.all_gather(hidden, 'tensor', axis=0, tiled=True)  34.6 us
    psum x1, waiting for transfers between devices, local(): down_sum, up_sum = lax.psum((down_own, up_own), 'tensor')  31.6 us
    dot_general x5, matrix products, contract_helper(): lax.dot_general(left, right, (((left_dim,), (right_dim,)), ((), ())), pre...  19.5 us
  transfers between devices with their start and end apart: 5, of which 5 were waited for; matrix products, arithmetic and copies ran while one was open for 8% of the time, Pallas kernels for 0%

commit v1 on v0

v1 whole, which is shorter than its diff:
```python
import functools

import jax
import jax.numpy as jnp
from jax import lax
from jax.experimental import pallas as pl
from jax.experimental.pallas import tpu as pltpu
from jax.sharding import PartitionSpec as P

RMIN = 8
PADDED_RANK = 64
MESH = pl.DeviceIdType.MESH
BF16 = jnp.bfloat16
F32 = jnp.float32

adapter_alpha_scale = 16.0
beta_one = 0.9
beta_two = 0.999
adam_eps = 1e-08
learn_rate = 0.0002
weight_decay = 0.1
first_fix = 0.9999734386011124
second_fix = 0.09520785288629038


def adamw(master, moment, second, grad):
    new_moment = beta_one * moment + (1.0 - beta_one) * grad
    new_second = beta_two * second + (1.0 - beta_two) * grad * grad
    update = new_moment / first_fix / (jnp.sqrt(new_second / second_fix) + adam_eps)
    new_master = master - learn_rate * (update + weight_decay * master)
    return (new_master, new_moment, new_second)


def dot_nn(left, right):
    return lax.dot_general(left, right, (((1,), (0,)), ((), ())), preferred_element_type=F32)


def dot_nt(left, right):
    return lax.dot_general(left, right, (((1,), (1,)), ((), ())), preferred_element_type=F32)


def kernel(
    D, T, R, W, C,
    tok_ref, bucket_ref, owner_ref, live_ref,
    hidden_hbm, cot_hbm, frozen_hbm, down_hbm, up_hbm,
    hgrad_ref, gdown_ref, gup_ref,
    cot, mc, upf, dfac, frozen, hid,
    lr, part, crecv, ysend, yrecv,
    up_placed, up_placed_t, down_placed_t,
    xsend, xrecv, gown, zsend, zrecv,
    load_sem, hs, hr, ls, lrs, cs, cr, ys, yr, xs, xr, zs, zr,
):
    K = PADDED_RANK
    S = D
    A = D // 2
    Y = T // 2
    r = R // T
    Wc = W // T
    NG = Wc // C
    p = lax.axis_index("dp")
    m = lax.axis_index("tensor")
    a, b = p // 2, p % 2
    y, c = m // 2, m % 2
    ob, oc = 1 - b, 1 - c

    tensor_peers = [(p, lax.rem(m + k, T)) for k in range(1, T)]
    x_peer = (a * 2 + ob, m)
    z_peers = [(lax.rem(a + k, A) * 2 + b, m) for k in range(1, A)]
    core_peer = (p, y * 2 + oc)
    y_peers = [(p, lax.rem(y + k, Y) * 2 + c) for k in range(1, Y)]

    def remote(src, dst, ssem, rsem, dev):
        return pltpu.make_async_remote_copy(
            src_ref=src, dst_ref=dst, send_sem=ssem, recv_sem=rsem,
            device_id=dev, device_id_type=MESH,
        )

    cot_load = pltpu.make_async_copy(cot_hbm, cot, load_sem.at[0])
    upf_load = pltpu.make_async_copy(up_hbm, upf, load_sem.at[1])
    cot_load.start()
    upf_load.start()
    frozen_loads = []
    for j in range(T):
        ld = pltpu.make_async_copy(
            frozen_hbm.at[pl.ds(j * Wc, Wc)], frozen.at[pl.ds(j * Wc, Wc)], load_sem.at[4 + j]
        )
        ld.start()
        frozen_loads.append(ld)
    dfac_load = pltpu.make_async_copy(down_hbm, dfac, load_sem.at[2])
    dfac_load.start()
    my_rows = pl.ds(pl.multiple_of(m * r, r), r)
    own_hid_load = pltpu.make_async_copy(
        hidden_hbm.at[:, pl.ds(pl.multiple_of(m * Wc, Wc), Wc)], hid.at[my_rows], load_sem.at[3]
    )
    own_hid_load.start()

    barrier = pltpu.get_barrier_semaphore()
    peers = tensor_peers + [x_peer] + z_peers
    for dev in peers:
        pl.semaphore_signal(barrier, inc=1, device_id=dev, device_id_type=MESH)
    pl.semaphore_wait(barrier, len(peers))

    hid_sends, hid_recvs = [], []
    for k in range(1, T):
        to = lax.rem(m + k, T)
        src = hidden_hbm.at[:, pl.ds(pl.multiple_of(to * Wc, Wc), Wc)]
        s = remote(src, hid.at[my_rows], hs.at[k - 1], hr.at[k - 1], (p, to))
        s.start()
        hid_sends.append(s)
        frm = lax.rem(m + T - k, T)
        hid_recvs.append(remote(
            src, hid.at[pl.ds(pl.multiple_of(frm * r, r), r)], hs.at[k - 1], hr.at[k - 1], (p, to)
        ))

    tok_col = jnp.broadcast_to(tok_ref[...].astype(F32), (128, R)).T.astype(jnp.int32)[:, :K]
    slot_of = jnp.zeros_like(tok_col)
    bucket = jnp.zeros_like(tok_col)
    for i in range(S):
        hit = tok_col == i
        slot_of = jnp.where(hit, owner_ref[i], slot_of)
        bucket = jnp.where(hit, bucket_ref[i], bucket)
    steps_up = (
        1
        + (bucket >= 1).astype(jnp.int32)
        + 2 * (bucket >= 2).astype(jnp.int32)
        + 4 * (bucket >= 3).astype(jnp.int32)
    )
    rank = RMIN * steps_up
    lane = lax.broadcasted_iota(jnp.int32, (R, K), 1)
    factor = jnp.where(lane < rank, adapter_alpha_scale / rank.astype(F32), 0.0)

    def own_slot(full):
        total = jnp.zeros((R, K), F32)
        for s in range(S):
            total = total + jnp.where(slot_of == s, full[:, s * K:(s + 1) * K], 0.0)
        return total

    def exchange(kind, own):
        lr[kind, m] = jnp.concatenate([own[: R // 2], own[R // 2:]], axis=1)
        out = []
        for k in range(1, T):
            s = remote(
                lr.at[kind, m], lr.at[kind, m], ls.at[kind, k - 1], lrs.at[kind, k - 1],
                (p, lax.rem(m + k, T)),
            )
            s.start()
            frm = lax.rem(m + T - k, T)
            out.append((s, remote(
                lr.at[kind, m], lr.at[kind, frm], ls.at[kind, k - 1], lrs.at[kind, k - 1],
                (p, lax.rem(m + k, T)),
            )))
        return out

    def gathered(kind, copies):
        for _, rcv in copies:
            rcv.wait_recv()
        total = lr[kind, 0]
        for i in range(1, T):
            total = total + lr[kind, i]
        own = jnp.concatenate([total[:, :K], total[:, K:]], axis=0)
        weight = (own * factor).astype(BF16).astype(F32)
        return jnp.concatenate([jnp.where(slot_of == s, weight, 0.0) for s in range(S)], axis=1)

    def place_transposed(ref, placed):
        turned = placed.T
        for s in range(S):
            ref[s % 2, pl.ds((s // 2) * K, K), :] = turned[s * K:(s + 1) * K].astype(BF16)

    cot_load.wait()
    row = lax.broadcasted_iota(jnp.int32, (R, C), 0)
    mc[...] = jnp.where(row < live_ref[p], cot[...].astype(F32), 0.0).astype(BF16)
    upf_load.wait()
    up_copies = exchange(0, own_slot(dot_nt(mc[...], upf[...])))

    tile = min(512, Wc)
    for j in range(T):
        frozen_loads[j].wait()

        def frozen_tile(t, carry, j=j):
            cols = pl.ds(pl.multiple_of(t * tile, tile), tile)
            rows = pl.ds(pl.multiple_of(j * Wc + t * tile, tile), tile)
            res = dot_nt(mc[...], frozen[rows, :])
            for i in range(T):
                part[j, i % 2, i // 2, :, cols] = res[i * r:(i + 1) * r]
            return carry

        lax.fori_loop(0, Wc // tile, frozen_tile, 0)

    placed = gathered(0, up_copies)
    up_placed[...] = placed.astype(BF16)
    place_transposed(up_placed_t, placed)
    dfac_load.wait()

    def extra_tile(t, carry):
        cols = pl.ds(pl.multiple_of(t * tile, tile), tile)
        res = dot_nt(up_placed[...], dfac[cols, :])
        for i in range(T):
            part[m, i % 2, i // 2, :, cols] += res[i * r:(i + 1) * r]
        return carry

    lax.fori_loop(0, Wc // tile, extra_tile, 0)

    core_copies = []
    for j in range(T):
        cp = remote(part.at[j, oc], crecv.at[j], cs.at[j], cr.at[j], core_peer)
        cp.start()
        core_copies.append(cp)

    own_hid_load.wait()
    for rcv in hid_recvs:
        rcv.wait_recv()

    x_copies = []

    def grad_chunk(i, left, right):
        xsend[i] = dot_nn(left[ob], right).astype(BF16).reshape(A, K, C)
        cp = remote(xsend.at[i], xrecv.at[i], xs.at[i], xr.at[i], x_peer)
        cp.start()
        x_copies.append(cp)
        gown[i] = dot_nn(left[b], right).reshape(A, K, C)

    grad_chunk(0, up_placed_t, hid[:, :C])
    down_part = dot_nn(hid[...], dfac[...])
    down_copies = exchange(1, own_slot(down_part))
    for i in range(1, NG):
        grad_chunk(i, up_placed_t, hid[:, i * C:(i + 1) * C])

    y_copies = []

    def core_sum(j):
        core_copies[j].wait_recv()
        for k in range(1, Y):
            to = lax.rem(y + k, Y)
            ysend[k - 1, j] = (part[j, c, to] + crecv[j, to]).astype(BF16)
            cp = remote(
                ysend.at[k - 1, j], yrecv.at[k - 1, j], ys.at[k - 1, j], yr.at[k - 1, j],
                y_peers[k - 1],
            )
            cp.start()
            y_copies.append(cp)
        part[j, c, y] = part[j, c, y] + crecv[j, y]

    z_copies = []

    def pair_sum(i):
        x_copies[i].wait_recv()
        for k in range(1, A):
            to = lax.rem(a + k, A)
            zsend[k - 1, i] = (gown[i, to] + xrecv[i, to].astype(F32)).astype(BF16)
            cp = remote(
                zsend.at[k - 1, i], zrecv.at[k - 1, i], zs.at[k - 1, i], zr.at[k - 1, i],
                z_peers[k - 1],
            )
            cp.start()
            z_copies.append(cp)

    for j in range(T):
        core_sum(j)
    pair_sum(0)
    place_transposed(down_placed_t, gathered(1, down_copies))
    grad_chunk(NG, down_placed_t, mc[...])
    for i in range(1, NG + 1):
        pair_sum(i)

    def last_grad(i):
        total = gown[i, a] + xrecv[i, a].astype(F32)
        for k in range(1, A):
            z_copies[i * (A - 1) + k - 1].wait_recv()
            total = total + zrecv[k - 1, i].astype(F32)
        return total / R

    for j in range(T):
        total = part[j, c, y]
        for k in range(1, Y):
            y_copies[j * (Y - 1) + k - 1].wait_recv()
            total = total + yrecv[k - 1, j].astype(F32)
        hgrad_ref[:, j * Wc:(j + 1) * Wc] = total.astype(BF16)
    for i in range(NG):
        gdown_ref[:, i * C:(i + 1) * C] = last_grad(i)
    gup_ref[...] = last_grad(NG)

    for s in hid_sends + core_copies + x_copies + z_copies + y_copies:
        s.wait_send()
    for s, _ in up_copies + down_copies:
        s.wait_send()


def local(
    hidden, cotangent, frozen_key_value, adapter_down_factors, adapter_up_factors,
    down_master_copy, down_first_moment, down_second_moment,
    up_master_copy, up_first_moment, up_second_moment,
    adapter_of_token, adapter_rank_bucket, adapter_owner_slot, live_token_counts,
):
    D, T = lax.axis_size("dp"), lax.axis_size("tensor")
    R, C = cotangent.shape
    W = hidden.shape[1]
    K = PADDED_RANK
    A, Y, r, Wc = D // 2, T // 2, R // T, W // T
    NG = Wc // C
    vmem = pl.BlockSpec(memory_space=pltpu.VMEM)
    smem = pl.BlockSpec(memory_space=pltpu.SMEM)
    anym = pl.BlockSpec(memory_space=pl.ANY)
    dma = pltpu.SemaphoreType.DMA
    V = pltpu.VMEM
    hidden_gradient, gdown_t, gup = pl.pallas_call(
        functools.partial(kernel, D, T, R, W, C),
        out_shape=(
            jax.ShapeDtypeStruct((r, W), BF16),
            jax.ShapeDtypeStruct((K, Wc), F32),
            jax.ShapeDtypeStruct((K, C), F32),
        ),
        in_specs=[vmem, smem, smem, smem] + [anym] * 5,
        out_specs=(vmem, vmem, vmem),
        scratch_shapes=[
            V((R, C), BF16), V((R, C), BF16), V((D * K, C), BF16), V((Wc, D * K), BF16),
            V((W, C), BF16), V((R, Wc), BF16),
            V((2, T, R // 2, 2 * K), F32),
            V((T, 2, Y, r, Wc), F32), V((T, Y, r, Wc), F32),
            V((Y - 1, T, r, Wc), BF16), V((Y - 1, T, r, Wc), BF16),
            V((R, D * K), BF16), V((2, A * K, R), BF16), V((2, A * K, R), BF16),
            V((NG + 1, A, K, C), BF16), V((NG + 1, A, K, C), BF16), V((NG + 1, A, K, C), F32),
            V((A - 1, NG + 1, K, C), BF16), V((A - 1, NG + 1, K, C), BF16),
            dma((4 + T,)), dma((T - 1,)), dma((T - 1,)), dma((2, T - 1)), dma((2, T - 1)),
            dma((T,)), dma((T,)), dma((Y - 1, T)), dma((Y - 1, T)),
            dma((NG + 1,)), dma((NG + 1,)), dma((A - 1, NG + 1)), dma((A - 1, NG + 1)),
        ],
        compiler_params=pltpu.CompilerParams(
            collective_id=0, has_side_effects=True, vmem_limit_bytes=58 * 2**20
        ),
        cost_estimate=pl.CostEstimate(
            flops=2 * R * C * W, bytes_accessed=2 * W * C, transcendentals=0
        ),
        name="lora_backward",
    )(
        adapter_of_token.reshape(1, R), adapter_rank_bucket, adapter_owner_slot, live_token_counts,
        hidden, cotangent, frozen_key_value, adapter_down_factors, adapter_up_factors,
    )
    new_d = adamw(down_master_copy.T, down_first_moment.T, down_second_moment.T, gdown_t)
    new_u = adamw(up_master_copy, up_first_moment, up_second_moment, gup)
    return (hidden_gradient, *(v.T for v in new_d), *new_u)


def solution(mesh):
    return jax.shard_map(
        local,
        mesh=mesh,
        in_specs=(
            P(("dp", "tensor"), None),
            P("dp", "tensor"),
            P(None, "tensor"),
            P("tensor", None),
            P(None, "tensor"),
            P("tensor", "dp"),
            P("tensor", "dp"),
            P("tensor", "dp"),
            P("dp", "tensor"),
            P("dp", "tensor"),
            P("dp", "tensor"),
            P("dp", None),
            P(),
            P(),
            P(),
        ),
        out_specs=(
            P(("dp", "tensor"), None),
            P("tensor", "dp"),
            P("tensor", "dp"),
            P("tensor", "dp"),
            P("dp", "tensor"),
            P("dp", "tensor"),
            P("dp", "tensor"),
        ),
        check_vma=False,
    )
```

time: 324 us -> 70.2 us (0.22)
  waiting for transfers between devices: 276 us -> 0 us
  Pallas kernels: 0 us -> 62.6 us
  matrix products: 21.6 us -> 0 us
  between operations: 13.9 us -> 0.72 us
  other arithmetic: 10.1 us -> 4.28 us
    reduce_scatter x3 -> x0, waiting for transfers between devices: 209 us -> none  [the longest x1 88.7 us: local(): lax.psum_scatter(grad_all_down, 'dp', scatter_dimension=1, tiled=True)]
    pallas_call x0 -> x1, Pallas kernels: none -> 62.6 us  [local(): pl.pallas_call(functools.partial(kernel, D, T, R, W, C), out_shape=(jax.S...]
    all_gather x1 -> x0, waiting for transfers between devices: 34.6 us -> none  [local(): gathered = lax.all_gather(hidden, 'tensor', axis=0, tiled=True)]
    psum x1 -> x0, waiting for transfers between devices: 31.6 us -> none  [local(): down_sum, up_sum = lax.psum((down_own, up_own), 'tensor')]
    dot_general x6 -> x0, matrix products: 21.6 us -> none  [the longest x5 19.5 us: contract_helper(): lax.dot_general(left, right, (((left_dim,), (right_dim,)), ((), ())), pre...]
    convert_element_type x2 -> x0, other arithmetic: 3.55 us -> none  [the longest x1 2.66 us: local(): hidden_gradient = reduced.astype(jnp.bfloat16)]
  transfers between devices with their start and end apart: 5 -> 0, of which waited for: 5 -> 0; matrix products, arithmetic and copies ran while one was open for 8% -> 0% of each run, Pallas kernels for 0% -> 0%
where the time goes in v1:
time: 70.2 us; the launch traced here: 69.9 us
  Pallas kernels  62.6 us (89%)
  other arithmetic  4.28 us (6%)
  local copies, waits for them, and re-layouts  2.29 us (3%)
  between operations  0.72 us (1%)
    pallas_call x1, Pallas kernels, local(): pl.pallas_call(functools.partial(kernel, D, T, R, W, C), out_shape=(jax.S...  62.6 us
    transpose x1, other arithmetic, local(): return (hidden_gradient, *(v.T for v in new_d), *new_u)  2.57 us
    unnamed x13, local copies, waits for them, and re-layouts  2.29 us
    sub x1, other arithmetic, adamw(): new_master = master - learn_rate * (update + weight_decay * master)  1.7 us

profile of v1, /device:TPU:0, one launch (start us, length us, event | category | flops | bytes accessed | tf_op | source)
XLA Modules:
  0.0 69.9 jit_solution(17200591239321535287)
XLA Ops:
  0.6 0.0 copy-start
  0.6 0.0 copy-start.1
  0.7 0.0 copy-start.2
  0.7 0.0 copy-start.3
  0.7 0.0 copy-start.4
  0.7 0.0 copy-start.5
  0.7 62.6 %lora_backward.1 = (bf16[64,8192]{1,0:T(8,128)(2,1)}, f32[64,2048]{1,0:T(8,128)}, f32[64,512]{1,0:T(8,128)}) custom-call(s32[1,256]{1,0:T(1,128)} %bitcast.30, s32[8]{0:T(128)} %bucket_ref.1, s32[8]{0:T(128)} %owner_ref.1, s32[8]{0:T(128)} %live_ref.1, bf16[64,8192]{1,0:T(8,128)(2,1)} %hidden_hbm.1, bf16[256,512]{1,0:T(8,128)(2,1)} %cot_hbm.1, ...), custom_call_target="tpu_custom_call" | custom-call | flops 2147483648 | bytes 8388608 | tf_op jit(solution)/shard_map/lora_backward/pallas_call | solution.py:305
  63.3 0.0 copy-done
  63.3 0.0 copy-done.1
  63.4 0.0 copy-done.2
  63.4 2.6 %fusion.5 = (f32[2048,64]{0,1:T(8,128)}, f32[2048,64]{0,1:T(8,128)}, f32[2048,64]{0,1:T(8,128)}) fusion(f32[64,2048]{1,0:T(8,128)} %get-tuple-element.11, f32[2048,64]{0,1:T(8,128)S(1)} %copy-done, f32[2048,64]{0,1:T(8,128)S(1)} %copy-done.1, f32[2048,64]{0,1:T(8,128)S(1)} %copy-done.2), kind=kLoop, calls=%fused_computation.10 | loop fusion | flops 1966080 | bytes 3670016 | tf_op jit(solution)/shard_map/transpose | solution.py:340
  65.9 0.0 copy-done.3
  65.9 0.0 copy-done.4
  65.9 0.0 copy-done.5
  65.9 1.7 %multiply_subtract_fusion = (f32[64,512]{1,0:T(8,128)}, f32[64,512]{1,0:T(8,128)}, f32[64,512]{1,0:T(8,128)}) fusion(f32[64,512]{1,0:T(8,128)S(1)} %copy-done.3, f32[64,512]{1,0:T(8,128)} %get-tuple-element.12, f32[64,512]{1,0:T(8,128)S(1)} %copy-done.4, f32[64,512]{1,0:T(8,128)S(1)} %copy-done.5), kind=kLoop, calls=%fused_computation.12 | loop fusion | flops 491520 | bytes 917504 | tf_op jit(solution)/shard_map/sub | solution.py:30
  67.7 2.3 %copy.23 = bf16[64,8192]{1,0:T(8,128)(2,1)} copy(bf16[64,8192]{1,0:T(8,128)(2,1)} %get-tuple-element.26) | data formatting | bytes 2097152
Async XLA Ops:
  0.6 62.7 %copy-start = (f32[2048,64]{0,1:T(8,128)S(1)}, f32[2048,64]{0,1:T(8,128)}, u32[]{:S(2)}) copy-start(f32[2048,64]{0,1:T(8,128)} %param.22) | copy-start | bytes 1572868
  0.6 62.7 %copy-start.1 = (f32[2048,64]{0,1:T(8,128)S(1)}, f32[2048,64]{0,1:T(8,128)}, u32[]{:S(2)}) copy-start(f32[2048,64]{0,1:T(8,128)} %param.21) | copy-start | bytes 1572868
  0.7 62.7 %copy-start.2 = (f32[2048,64]{0,1:T(8,128)S(1)}, f32[2048,64]{0,1:T(8,128)}, u32[]{:S(2)}) copy-start(f32[2048,64]{0,1:T(8,128)} %param.20) | copy-start | bytes 1572868
  0.7 65.3 %copy-start.3 = (f32[64,512]{1,0:T(8,128)S(1)}, f32[64,512]{1,0:T(8,128)}, u32[]{:S(2)}) copy-start(f32[64,512]{1,0:T(8,128)} %param.23) | copy-start | bytes 393220
  0.7 65.3 %copy-start.4 = (f32[64,512]{1,0:T(8,128)S(1)}, f32[64,512]{1,0:T(8,128)}, u32[]{:S(2)}) copy-start(f32[64,512]{1,0:T(8,128)} %param.24) | copy-start | bytes 393220
  0.7 65.3 %copy-start.5 = (f32[64,512]{1,0:T(8,128)S(1)}, f32[64,512]{1,0:T(8,128)}, u32[]{:S(2)}) copy-start(f32[64,512]{1,0:T(8,128)} %param.25) | copy-start | bytes 393220

commit v2 on v1

--- a/solution.py
+++ b/solution.py
@@ -79,38 +79,29 @@
     upf_load = pltpu.make_async_copy(up_hbm, upf, load_sem.at[1])
     cot_load.start()
     upf_load.start()
+    order = [lax.rem(2 * (y + 1) + i, T) for i in range(T)]
     frozen_loads = []
-    for j in range(T):
-        ld = pltpu.make_async_copy(
-            frozen_hbm.at[pl.ds(j * Wc, Wc)], frozen.at[pl.ds(j * Wc, Wc)], load_sem.at[4 + j]
-        )
+    for i, j in enumerate(order):
+        rows = pl.ds(pl.multiple_of(j * Wc, Wc), Wc)
+        ld = pltpu.make_async_copy(frozen_hbm.at[rows], frozen.at[rows], load_sem.at[4 + i])
         ld.start()
         frozen_loads.append(ld)
     dfac_load = pltpu.make_async_copy(down_hbm, dfac, load_sem.at[2])
     dfac_load.start()
     my_rows = pl.ds(pl.multiple_of(m * r, r), r)
-    own_hid_load = pltpu.make_async_copy(
-        hidden_hbm.at[:, pl.ds(pl.multiple_of(m * Wc, Wc), Wc)], hid.at[my_rows], load_sem.at[3]
-    )
-    own_hid_load.start()
+    own_hid_loads = []
+    for i in range(NG):
+        ld = pltpu.make_async_copy(
+            hidden_hbm.at[:, pl.ds(pl.multiple_of(m * Wc + i * C, C), C)], hid.at[i, my_rows],
+            load_sem.at[4 + T + i],
+        )
+        ld.start()
+        own_hid_loads.append(ld)
 
     barrier = pltpu.get_barrier_semaphore()
     peers = tensor_peers + [x_peer] + z_peers
     for dev in peers:
         pl.semaphore_signal(barrier, inc=1, device_id=dev, device_id_type=MESH)
-    pl.semaphore_wait(barrier, len(peers))
-
-    hid_sends, hid_recvs = [], []
-    for k in range(1, T):
-        to = lax.rem(m + k, T)
-        src = hidden_hbm.at[:, pl.ds(pl.multiple_of(to * Wc, Wc), Wc)]
-        s = remote(src, hid.at[my_rows], hs.at[k - 1], hr.at[k - 1], (p, to))
-        s.start()
-        hid_sends.append(s)
-        frm = lax.rem(m + T - k, T)
-        hid_recvs.append(remote(
-            src, hid.at[pl.ds(pl.multiple_of(frm * r, r), r)], hs.at[k - 1], hr.at[k - 1], (p, to)
-        ))
 
     tok_col = jnp.broadcast_to(tok_ref[...].astype(F32), (128, R)).T.astype(jnp.int32)[:, :K]
     slot_of = jnp.zeros_like(tok_col)
@@ -170,45 +161,55 @@
     row = lax.broadcasted_iota(jnp.int32, (R, C), 0)
     mc[...] = jnp.where(row < live_ref[p], cot[...].astype(F32), 0.0).astype(BF16)
     upf_load.wait()
-    up_copies = exchange(0, own_slot(dot_nt(mc[...], upf[...])))
+    up_own = own_slot(dot_nt(mc[...], upf[...]))
+    pl.semaphore_wait(barrier, len(peers))
+    up_copies = exchange(0, up_own)
+
+    hid_sends, hid_recvs = [], []
+    for i in range(NG):
+        recvs = []
+        for k in range(1, T):
+            to = lax.rem(m + k, T)
+            frm = lax.rem(m + T - k, T)
+            src = hidden_hbm.at[:, pl.ds(pl.multiple_of(to * Wc + i * C, C), C)]
+            sems = (hs.at[k - 1, i], hr.at[k - 1, i], (p, to))
+            s = remote(src, hid.at[i, my_rows], *sems)
+            s.start()
+            hid_sends.append(s)
+            recvs.append(remote(src, hid.at[i, pl.ds(pl.multiple_of(frm * r, r), r)], *sems))
+        hid_recvs.append(recvs)
 
     tile = min(512, Wc)
-    for j in range(T):
-        frozen_loads[j].wait()
-
-        def frozen_tile(t, carry, j=j):
+
+    def frozen_chunk(i):
+        j = order[i]
+        frozen_loads[i].wait()
+
+        def frozen_tile(t, carry):
             cols = pl.ds(pl.multiple_of(t * tile, tile), tile)
             rows = pl.ds(pl.multiple_of(j * Wc + t * tile, tile), tile)
             res = dot_nt(mc[...], frozen[rows, :])
-            for i in range(T):
-                part[j, i % 2, i // 2, :, cols] = res[i * r:(i + 1) * r]
+            for q in range(T):
+                part[j, q % 2, q // 2, :, cols] = res[q * r:(q + 1) * r]
             return carry
 
         lax.fori_loop(0, Wc // tile, frozen_tile, 0)
+
+    core_copies = []
+
+    def core_send(i):
+        j = order[i]
+        cp = remote(part.at[j, oc], crecv.at[j], cs.at[i], cr.at[i], core_peer)
+        cp.start()
+        core_copies.append(cp)
+
+    for i in range(T - 2):
+        frozen_chunk(i)
+        core_send(i)
 
     placed = gathered(0, up_copies)
     up_placed[...] = placed.astype(BF16)
     place_transposed(up_placed_t, placed)
-    dfac_load.wait()
-
-    def extra_tile(t, carry):
-        cols = pl.ds(pl.multiple_of(t * tile, tile), tile)
-        res = dot_nt(up_placed[...], dfac[cols, :])
-        for i in range(T):
-            part[m, i % 2, i // 2, :, cols] += res[i * r:(i + 1) * r]
-        return carry
-
-    lax.fori_loop(0, Wc // tile, extra_tile, 0)
-
-    core_copies = []
-    for j in range(T):
-        cp = remote(part.at[j, oc], crecv.at[j], cs.at[j], cr.at[j], core_peer)
-        cp.start()
-        core_copies.append(cp)
-
-    own_hid_load.wait()
-    for rcv in hid_recvs:
-        rcv.wait_recv()
 
     x_copies = []
 
@@ -219,16 +220,17 @@
         x_copies.append(cp)
         gown[i] = dot_nn(left[b], right).reshape(A, K, C)
 
-    grad_chunk(0, up_placed_t, hid[:, :C])
-    down_part = dot_nn(hid[...], dfac[...])
-    down_copies = exchange(1, own_slot(down_part))
-    for i in range(1, NG):
-        grad_chunk(i, up_placed_t, hid[:, i * C:(i + 1) * C])
+    def down_grad_chunk(i):
+        own_hid_loads[i].wait()
+        for rcv in hid_recvs[i]:
+            rcv.wait_recv()
+        grad_chunk(i, up_placed_t, hid[i])
 
     y_copies = []
 
-    def core_sum(j):
-        core_copies[j].wait_recv()
+    def core_sum(i):
+        j = order[i]
+        core_copies[i].wait_recv()
         for k in range(1, Y):
             to = lax.rem(y + k, Y)
             ysend[k - 1, j] = (part[j, c, to] + crecv[j, to]).astype(BF16)
@@ -254,8 +256,30 @@
             cp.start()
             z_copies.append(cp)
 
-    for j in range(T):
-        core_sum(j)
+    dfac_load.wait()
+    for i in range(T - 2, T):
+        frozen_chunk(i)
+
+    def extra_tile(t, carry):
+        cols = pl.ds(pl.multiple_of(t * tile, tile), tile)
+        res = dot_nt(up_placed[...], dfac[cols, :])
+        for q in range(T):
+            part[m, q % 2, q // 2, :, cols] += res[q * r:(q + 1) * r]
+        return carry
+
+    down_grad_chunk(0)
+    lax.fori_loop(0, Wc // tile, extra_tile, 0)
+    for i in range(T - 2, T):
+        core_send(i)
+    core_sum(0)
+    for i in range(1, NG):
+        down_grad_chunk(i)
+    down_part = dot_nn(hid[0], dfac[:C, :])
+    for i in range(1, NG):
+        down_part = down_part + dot_nn(hid[i], dfac[i * C:(i + 1) * C, :])
+    down_copies = exchange(1, own_slot(down_part))
+    for i in range(1, T):
+        core_sum(i)
     pair_sum(0)
     place_transposed(down_placed_t, gathered(1, down_copies))
     grad_chunk(NG, down_placed_t, mc[...])
@@ -272,7 +296,10 @@
     for j in range(T):
         total = part[j, c, y]
         for k in range(1, Y):
-            y_copies[j * (Y - 1) + k - 1].wait_recv()
+            remote(
+                ysend.at[k - 1, j], yrecv.at[k - 1, j], ys.at[k - 1, j], yr.at[k - 1, j],
+                y_peers[k - 1],
+            ).wait_recv()
             total = total + yrecv[k - 1, j].astype(F32)
         hgrad_ref[:, j * Wc:(j + 1) * Wc] = total.astype(BF16)
     for i in range(NG):
@@ -283,6 +310,48 @@
         s.wait_send()
     for s, _ in up_copies + down_copies:
         s.wait_send()
+
+
+def tail_kernel(*refs):
+    hgrad_hbm, grad_d, grad_u = refs[0], refs[1], refs[2]
+    down_in, up_in = refs[3:6], refs[6:9]
+    hout_hbm, down_out, up_out, sem = refs[9], refs[10:13], refs[13:16], refs[16]
+    copy = pltpu.make_async_copy(hgrad_hbm, hout_hbm, sem)
+
+    @pl.when(pl.program_id(0) == 0)
+    def _():
+        copy.start()
+
+    for ins, grad, outs in ((down_in, grad_d, down_out), (up_in, grad_u, up_out)):
+        for ref, value in zip(outs, adamw(*(v[...] for v in ins), grad[...])):
+            ref[...] = value
+
+    @pl.when(pl.program_id(0) == pl.num_programs(0) - 1)
+    def _():
+        copy.wait()
+
+
+def tail(hgrad, grad_d, grad_u, down, up):
+    K, Wc = grad_d.shape
+    C = grad_u.shape[1]
+    steps = 4
+    anym = pl.BlockSpec(memory_space=pl.ANY)
+    big = pl.BlockSpec((K // steps, Wc), lambda i: (i, 0))
+    small = pl.BlockSpec((K // steps, C), lambda i: (i, 0))
+    return pl.pallas_call(
+        tail_kernel,
+        grid=(steps,),
+        out_shape=(
+            jax.ShapeDtypeStruct(hgrad.shape, hgrad.dtype),
+            *(jax.ShapeDtypeStruct((K, Wc), F32),) * 3,
+            *(jax.ShapeDtypeStruct((K, C), F32),) * 3,
+        ),
+        in_specs=[anym, big, small, big, big, big, small, small, small],
+        out_specs=(anym, big, big, big, small, small, small),
+        scratch_shapes=[pltpu.SemaphoreType.DMA],
+        cost_estimate=pl.CostEstimate(flops=0, bytes_accessed=8 * K * Wc * 4, transcendentals=0),
+        name="adamw_tail",
+    )(hgrad, grad_d, grad_u, *down, *up)
 
 
 def local(
@@ -313,14 +382,14 @@
         out_specs=(vmem, vmem, vmem),
         scratch_shapes=[
             V((R, C), BF16), V((R, C), BF16), V((D * K, C), BF16), V((Wc, D * K), BF16),
-            V((W, C), BF16), V((R, Wc), BF16),
+            V((W, C), BF16), V((NG, R, C), BF16),
             V((2, T, R // 2, 2 * K), F32),
             V((T, 2, Y, r, Wc), F32), V((T, Y, r, Wc), F32),
             V((Y - 1, T, r, Wc), BF16), V((Y - 1, T, r, Wc), BF16),
             V((R, D * K), BF16), V((2, A * K, R), BF16), V((2, A * K, R), BF16),
             V((NG + 1, A, K, C), BF16), V((NG + 1, A, K, C), BF16), V((NG + 1, A, K, C), F32),
             V((A - 1, NG + 1, K, C), BF16), V((A - 1, NG + 1, K, C), BF16),
-            dma((4 + T,)), dma((T - 1,)), dma((T - 1,)), dma((2, T - 1)), dma((2, T - 1)),
+            dma((4 + T + NG,)), dma((T - 1, NG)), dma((T - 1, NG)), dma((2, T - 1)), dma((2, T - 1)),
             dma((T,)), dma((T,)), dma((Y - 1, T)), dma((Y - 1, T)),
             dma((NG + 1,)), dma((NG + 1,)), dma((A - 1, NG + 1)), dma((A - 1, NG + 1)),
         ],
@@ -335,9 +404,12 @@
         adapter_of_token.reshape(1, R), adapter_rank_bucket, adapter_owner_slot, live_token_counts,
         hidden, cotangent, frozen_key_value, adapter_down_factors, adapter_up_factors,
     )
-    new_d = adamw(down_master_copy.T, down_first_moment.T, down_second_moment.T, gdown_t)
-    new_u = adamw(up_master_copy, up_first_moment, up_second_moment, gup)
-    return (hidden_gradient, *(v.T for v in new_d), *new_u)
+    hidden_gradient, *new = tail(
+        hidden_gradient, gdown_t, gup,
+        (down_master_copy.T, down_first_moment.T, down_second_moment.T),
+        (up_master_copy, up_first_moment, up_second_moment),
+    )
+    return (hidden_gradient, *(v.T for v in new[:3]), *new[3:])
 
 
 def solution(mesh):

time: 70.2 us -> 92 us (1.31)
  Pallas kernels: 62.6 us -> 90.3 us
  other arithmetic: 4.28 us -> 0 us
  local copies, waits for them, and re-layouts: 2.29 us -> 0 us
    pallas_call x0 -> x1, Pallas kernels: none -> 34.8 us  [tail(): pl.pallas_call(tail_kernel, grid=(steps,), out_shape=(jax.ShapeDtypeStruc...]
    pallas_call x1, Pallas kernels: 62.6 us -> 55.5 us  [local(): pl.pallas_call(functools.partial(kernel, D, T, R, W, C), out_shape=(jax.S...]
    transpose x1 -> x0, other arithmetic: 2.57 us -> none  [local(): return (hidden_gradient, *(v.T for v in new_d), *new_u)]
    unnamed x13 -> x0, local copies, waits for them, and re-layouts: 2.29 us -> none
    sub x1 -> x0, other arithmetic: 1.7 us -> none  [adamw(): new_master = master - learn_rate * (update + weight_decay * master)]
where the time goes in v2:
time: 92 us; the launch traced here: 90.9 us
  Pallas kernels  90.3 us (98%)
    pallas_call x1, Pallas kernels, local(): pl.pallas_call(functools.partial(kernel, D, T, R, W, C), out_shape=(jax.S...  55.5 us
    pallas_call x1, Pallas kernels, tail(): pl.pallas_call(tail_kernel, grid=(steps,), out_shape=(jax.ShapeDtypeStruc...  34.8 us

profile of v2, /device:TPU:0, one launch (start us, length us, event | category | flops | bytes accessed | tf_op | source)
XLA Modules:
  0.0 90.9 jit_solution(2356174710957801710)
XLA Ops:
  0.6 55.5 %lora_backward.1 = (bf16[64,8192]{1,0:T(8,128)(2,1)}, f32[64,2048]{1,0:T(8,128)}, f32[64,512]{1,0:T(8,128)}) custom-call(s32[1,256]{1,0:T(1,128)} %bitcast.10, s32[8]{0:T(128)} %bucket_ref.1, s32[8]{0:T(128)} %owner_ref.1, s32[8]{0:T(128)} %live_ref.1, bf16[64,8192]{1,0:T(8,128)(2,1)} %hidden_hbm.1, bf16[256,512]{1,0:T(8,128)(2,1)} %cot_hbm.1, ...), custom_call_target="tpu_custom_call" | custom-call | flops 2147483648 | bytes 8388608 | tf_op jit(solution)/shard_map/lora_backward/pallas_call | solution.py:374
  56.1 34.8 %adamw_tail.1 = (bf16[64,8192]{1,0:T(8,128)(2,1)}, f32[64,2048]{1,0:T(8,128)}, f32[64,2048]{1,0:T(8,128)}, f32[64,2048]{1,0:T(8,128)}, f32[64,512]{1,0:T(8,128)}, /*index=5*/f32[64,512]{1,0:T(8,128)}, f32[64,512]{1,0:T(8,128)}) custom-call(bf16[64,8192]{1,0:T(8,128)(2,1)} %get-tuple-element.17.refs_0_, f32[64,2048]{1,0:T(8,128)} %get-tuple-element.18.refs_1_, ...), custom_call_target="tpu_custom_call" | custom-call | bytes 4194304 | tf_op jit(solution)/shard_map/adamw_tail/pallas_call | solution.py:341

commit v3 on v2

--- a/solution.py
+++ b/solution.py
@@ -44,11 +44,11 @@
     tok_ref, bucket_ref, owner_ref, live_ref,
     hidden_hbm, cot_hbm, frozen_hbm, down_hbm, up_hbm,
     hgrad_ref, gdown_ref, gup_ref,
-    cot, mc, upf, dfac, frozen, hid,
-    lr, part, crecv, ysend, yrecv,
+    cot, mc, upf, dfac, frozen, hidv, hid,
+    lr_c, lr_y, part, crecv, ysend, yrecv,
     up_placed, up_placed_t, down_placed_t,
     xsend, xrecv, gown, zsend, zrecv,
-    load_sem, hs, hr, ls, lrs, cs, cr, ys, yr, xs, xr, zs, zr,
+    load_sem, hs, hr, lcs, lcr, lys, lyr, cs, cr, ys, yr, xs, xr, zs, zr,
 ):
     K = PADDED_RANK
     S = D
@@ -56,7 +56,9 @@
     Y = T // 2
     r = R // T
     Wc = W // T
-    NG = Wc // C
+    Q = C // 2
+    NG = Wc // Q
+    NU = C // Q
     p = lax.axis_index("dp")
     m = lax.axis_index("tensor")
     a, b = p // 2, p % 2
@@ -79,6 +81,8 @@
     upf_load = pltpu.make_async_copy(up_hbm, upf, load_sem.at[1])
     cot_load.start()
     upf_load.start()
+    hid_load = pltpu.make_async_copy(hidden_hbm, hidv, load_sem.at[3])
+    hid_load.start()
     order = [lax.rem(2 * (y + 1) + i, T) for i in range(T)]
     frozen_loads = []
     for i, j in enumerate(order):
@@ -89,15 +93,6 @@
     dfac_load = pltpu.make_async_copy(down_hbm, dfac, load_sem.at[2])
     dfac_load.start()
     my_rows = pl.ds(pl.multiple_of(m * r, r), r)
-    own_hid_loads = []
-    for i in range(NG):
-        ld = pltpu.make_async_copy(
-            hidden_hbm.at[:, pl.ds(pl.multiple_of(m * Wc + i * C, C), C)], hid.at[i, my_rows],
-            load_sem.at[4 + T + i],
-        )
-        ld.start()
-        own_hid_loads.append(ld)
-
     barrier = pltpu.get_barrier_semaphore()
     peers = tensor_peers + [x_peer] + z_peers
     for dev in peers:
@@ -126,28 +121,36 @@
             total = total + jnp.where(slot_of == s, full[:, s * K:(s + 1) * K], 0.0)
         return total
 
-    def exchange(kind, own):
-        lr[kind, m] = jnp.concatenate([own[: R // 2], own[R // 2:]], axis=1)
-        out = []
-        for k in range(1, T):
-            s = remote(
-                lr.at[kind, m], lr.at[kind, m], ls.at[kind, k - 1], lrs.at[kind, k - 1],
-                (p, lax.rem(m + k, T)),
-            )
+    lr_sends = []
+
+    def core_exchange(kind, own):
+        lr_c[kind, 0] = jnp.concatenate([own[: R // 2], own[R // 2:]], axis=1)
+        cp = remote(
+            lr_c.at[kind, 0], lr_c.at[kind, 1], lcs.at[kind], lcr.at[kind], core_peer
+        )
+        cp.start()
+        lr_sends.append(cp)
+        return cp
+
+    def y_exchange(kind, cp):
+        cp.wait_recv()
+        lr_y[kind, y] = lr_c[kind, 0] + lr_c[kind, 1]
+        recvs = []
+        for k in range(1, Y):
+            frm = lax.rem(y + Y - k, Y)
+            sems = (lys.at[kind, k - 1], lyr.at[kind, k - 1], y_peers[k - 1])
+            s = remote(lr_y.at[kind, y], lr_y.at[kind, y], *sems)
             s.start()
-            frm = lax.rem(m + T - k, T)
-            out.append((s, remote(
-                lr.at[kind, m], lr.at[kind, frm], ls.at[kind, k - 1], lrs.at[kind, k - 1],
-                (p, lax.rem(m + k, T)),
-            )))
-        return out
-
-    def gathered(kind, copies):
-        for _, rcv in copies:
+            lr_sends.append(s)
+            recvs.append(remote(lr_y.at[kind, y], lr_y.at[kind, frm], *sems))
+        return recvs
+
+    def gathered(kind, recvs):
+        for rcv in recvs:
             rcv.wait_recv()
-        total = lr[kind, 0]
-        for i in range(1, T):
-            total = total + lr[kind, i]
+        total = lr_y[kind, 0]
+        for i in range(1, Y):
+            total = total + lr_y[kind, i]
         own = jnp.concatenate([total[:, :K], total[:, K:]], axis=0)
         weight = (own * factor).astype(BF16).astype(F32)
         return jnp.concatenate([jnp.where(slot_of == s, weight, 0.0) for s in range(S)], axis=1)
@@ -163,21 +166,29 @@
     upf_load.wait()
     up_own = own_slot(dot_nt(mc[...], upf[...]))
     pl.semaphore_wait(barrier, len(peers))
-    up_copies = exchange(0, up_own)
-
+    up_core = core_exchange(0, up_own)
+
+    hid_load.wait()
     hid_sends, hid_recvs = [], []
-    for i in range(NG):
+
+    def send_hidden(i):
         recvs = []
         for k in range(1, T):
             to = lax.rem(m + k, T)
             frm = lax.rem(m + T - k, T)
-            src = hidden_hbm.at[:, pl.ds(pl.multiple_of(to * Wc + i * C, C), C)]
+            src = hidv.at[:, pl.ds(pl.multiple_of(to * Wc + i * Q, Q), Q)]
             sems = (hs.at[k - 1, i], hr.at[k - 1, i], (p, to))
             s = remote(src, hid.at[i, my_rows], *sems)
             s.start()
             hid_sends.append(s)
             recvs.append(remote(src, hid.at[i, pl.ds(pl.multiple_of(frm * r, r), r)], *sems))
         hid_recvs.append(recvs)
+        hid[i, my_rows] = hidv[:, pl.ds(pl.multiple_of(m * Wc + i * Q, Q), Q)]
+
+    send_hidden(0)
+    up_recvs = y_exchange(0, up_core)
+    for i in range(1, NG):
+        send_hidden(i)
 
     tile = min(512, Wc)
 
@@ -207,21 +218,20 @@
         frozen_chunk(i)
         core_send(i)
 
-    placed = gathered(0, up_copies)
+    placed = gathered(0, up_recvs)
     up_placed[...] = placed.astype(BF16)
     place_transposed(up_placed_t, placed)
 
     x_copies = []
 
     def grad_chunk(i, left, right):
-        xsend[i] = dot_nn(left[ob], right).astype(BF16).reshape(A, K, C)
+        xsend[i] = dot_nn(left[ob], right).astype(BF16).reshape(A, K, Q)
         cp = remote(xsend.at[i], xrecv.at[i], xs.at[i], xr.at[i], x_peer)
         cp.start()
         x_copies.append(cp)
-        gown[i] = dot_nn(left[b], right).reshape(A, K, C)
+        gown[i] = dot_nn(left[b], right).reshape(A, K, Q)
 
     def down_grad_chunk(i):
-        own_hid_loads[i].wait()
         for rcv in hid_recvs[i]:
             rcv.wait_recv()
         grad_chunk(i, up_placed_t, hid[i])
@@ -274,16 +284,19 @@
     core_sum(0)
     for i in range(1, NG):
         down_grad_chunk(i)
-    down_part = dot_nn(hid[0], dfac[:C, :])
+    down_part = dot_nn(hid[0], dfac[:Q, :])
     for i in range(1, NG):
-        down_part = down_part + dot_nn(hid[i], dfac[i * C:(i + 1) * C, :])
-    down_copies = exchange(1, own_slot(down_part))
+        down_part = down_part + dot_nn(hid[i], dfac[i * Q:(i + 1) * Q, :])
+    down_core = core_exchange(1, own_slot(down_part))
+    pair_sum(0)
+    down_recvs = y_exchange(1, down_core)
     for i in range(1, T):
         core_sum(i)
-    pair_sum(0)
-    place_transposed(down_placed_t, gathered(1, down_copies))
-    grad_chunk(NG, down_placed_t, mc[...])
-    for i in range(1, NG + 1):
+        pair_sum(i)
+    place_transposed(down_placed_t, gathered(1, down_recvs))
+    for i in range(NU):
+        grad_chunk(NG + i, down_placed_t, mc[:, i * Q:(i + 1) * Q])
+    for i in range(T, NG + NU):
         pair_sum(i)
 
     def last_grad(i):
@@ -303,39 +316,29 @@
             total = total + yrecv[k - 1, j].astype(F32)
         hgrad_ref[:, j * Wc:(j + 1) * Wc] = total.astype(BF16)
     for i in range(NG):
-        gdown_ref[:, i * C:(i + 1) * C] = last_grad(i)
-    gup_ref[...] = last_grad(NG)
-
-    for s in hid_sends + core_copies + x_copies + z_copies + y_copies:
+        gdown_ref[:, i * Q:(i + 1) * Q] = last_grad(i)
+    for i in range(NU):
+        gup_ref[:, i * Q:(i + 1) * Q] = last_grad(NG + i)
+
+    for s in hid_sends + lr_sends + core_copies + x_copies + z_copies + y_copies:
         s.wait_send()
-    for s, _ in up_copies + down_copies:
-        s.wait_send()
 
 
 def tail_kernel(*refs):
-    hgrad_hbm, grad_d, grad_u = refs[0], refs[1], refs[2]
+    hgrad, grad_d, grad_u = refs[:3]
     down_in, up_in = refs[3:6], refs[6:9]
-    hout_hbm, down_out, up_out, sem = refs[9], refs[10:13], refs[13:16], refs[16]
-    copy = pltpu.make_async_copy(hgrad_hbm, hout_hbm, sem)
-
-    @pl.when(pl.program_id(0) == 0)
-    def _():
-        copy.start()
-
+    hout, down_out, up_out = refs[9], refs[10:13], refs[13:16]
+    hout[...] = hgrad[...]
     for ins, grad, outs in ((down_in, grad_d, down_out), (up_in, grad_u, up_out)):
         for ref, value in zip(outs, adamw(*(v[...] for v in ins), grad[...])):
             ref[...] = value
-
-    @pl.when(pl.program_id(0) == pl.num_programs(0) - 1)
-    def _():
-        copy.wait()
 
 
 def tail(hgrad, grad_d, grad_u, down, up):
     K, Wc = grad_d.shape
     C = grad_u.shape[1]
     steps = 4
-    anym = pl.BlockSpec(memory_space=pl.ANY)
+    wide = pl.BlockSpec((hgrad.shape[0], hgrad.shape[1] // steps), lambda i: (0, i))
     big = pl.BlockSpec((K // steps, Wc), lambda i: (i, 0))
     small = pl.BlockSpec((K // steps, C), lambda i: (i, 0))
     return pl.pallas_call(
@@ -346,9 +349,8 @@
             *(jax.ShapeDtypeStruct((K, Wc), F32),) * 3,
             *(jax.ShapeDtypeStruct((K, C), F32),) * 3,
         ),
-        in_specs=[anym, big, small, big, big, big, small, small, small],
-        out_specs=(anym, big, big, big, small, small, small),
-        scratch_shapes=[pltpu.SemaphoreType.DMA],
+        in_specs=[wide, big, small, big, big, big, small, small, small],
+        out_specs=(wide, big, big, big, small, small, small),
         cost_estimate=pl.CostEstimate(flops=0, bytes_accessed=8 * K * Wc * 4, transcendentals=0),
         name="adamw_tail",
     )(hgrad, grad_d, grad_u, *down, *up)
@@ -365,7 +367,9 @@
     W = hidden.shape[1]
     K = PADDED_RANK
     A, Y, r, Wc = D // 2, T // 2, R // T, W // T
-    NG = Wc // C
+    Q = C // 2
+    NG = Wc // Q
+    NC = NG + C // Q
     vmem = pl.BlockSpec(memory_space=pltpu.VMEM)
     smem = pl.BlockSpec(memory_space=pltpu.SMEM)
     anym = pl.BlockSpec(memory_space=pl.ANY)
@@ -382,16 +386,17 @@
         out_specs=(vmem, vmem, vmem),
         scratch_shapes=[
             V((R, C), BF16), V((R, C), BF16), V((D * K, C), BF16), V((Wc, D * K), BF16),
-            V((W, C), BF16), V((NG, R, C), BF16),
-            V((2, T, R // 2, 2 * K), F32),
+            V((W, C), BF16), V((r, W), BF16), V((NG, R, Q), BF16),
+            V((2, 2, R // 2, 2 * K), F32), V((2, Y, R // 2, 2 * K), F32),
             V((T, 2, Y, r, Wc), F32), V((T, Y, r, Wc), F32),
             V((Y - 1, T, r, Wc), BF16), V((Y - 1, T, r, Wc), BF16),
             V((R, D * K), BF16), V((2, A * K, R), BF16), V((2, A * K, R), BF16),
-            V((NG + 1, A, K, C), BF16), V((NG + 1, A, K, C), BF16), V((NG + 1, A, K, C), F32),
-            V((A - 1, NG + 1, K, C), BF16), V((A - 1, NG + 1, K, C), BF16),
-            dma((4 + T + NG,)), dma((T - 1, NG)), dma((T - 1, NG)), dma((2, T - 1)), dma((2, T - 1)),
+            V((NC, A, K, Q), BF16), V((NC, A, K, Q), BF16), V((NC, A, K, Q), F32),
+            V((A - 1, NC, K, Q), BF16), V((A - 1, NC, K, Q), BF16),
+            dma((4 + T,)), dma((T - 1, NG)), dma((T - 1, NG)),
+            dma((2,)), dma((2,)), dma((2, Y - 1)), dma((2, Y - 1)),
             dma((T,)), dma((T,)), dma((Y - 1, T)), dma((Y - 1, T)),
-            dma((NG + 1,)), dma((NG + 1,)), dma((A - 1, NG + 1)), dma((A - 1, NG + 1)),
+            dma((NC,)), dma((NC,)), dma((A - 1, NC)), dma((A - 1, NC)),
         ],
         compiler_params=pltpu.CompilerParams(
             collective_id=0, has_side_effects=True, vmem_limit_bytes=58 * 2**20

time: 92 us -> 59.1 us (0.64)
  Pallas kernels: 90.3 us -> 58.2 us
    pallas_call x1, Pallas kernels: 34.8 us -> 4.37 us  [tail(): pl.pallas_call(tail_kernel, grid=(steps,), out_shape=(jax.ShapeDtypeStruc...]
    pallas_call x1, Pallas kernels: 55.5 us -> 53.8 us  [local(): pl.pallas_call(functools.partial(kernel, D, T, R, W, C), out_shape=(jax.S...]
where the time goes in v3:
time: 59.1 us; the launch traced here: 58.9 us
  Pallas kernels  58.2 us (98%)
  between operations  0.64 us (1%)
    pallas_call x1, Pallas kernels, local(): pl.pallas_call(functools.partial(kernel, D, T, R, W, C), out_shape=(jax.S...  53.8 us
    pallas_call x1, Pallas kernels, tail(): pl.pallas_call(tail_kernel, grid=(steps,), out_shape=(jax.ShapeDtypeStruc...  4.37 us

profile of v3, /device:TPU:0, one launch (start us, length us, event | category | flops | bytes accessed | tf_op | source)
XLA Modules:
  0.0 58.9 jit_solution(12997969716044756297)
XLA Ops:
  0.6 53.8 %lora_backward.1 = (bf16[64,8192]{1,0:T(8,128)(2,1)}, f32[64,2048]{1,0:T(8,128)}, f32[64,512]{1,0:T(8,128)}) custom-call(s32[1,256]{1,0:T(1,128)} %bitcast.10, s32[8]{0:T(128)} %bucket_ref.1, s32[8]{0:T(128)} %owner_ref.1, s32[8]{0:T(128)} %live_ref.1, bf16[64,8192]{1,0:T(8,128)(2,1)} %hidden_hbm.1, bf16[256,512]{1,0:T(8,128)(2,1)} %cot_hbm.1, ...), custom_call_target="tpu_custom_call" | custom-call | flops 2147483648 | bytes 8388608 | tf_op jit(solution)/shard_map/lora_backward/pallas_call | solution.py:378
  54.5 4.4 %adamw_tail.1 = (bf16[64,8192]{1,0:T(8,128)(2,1)}, f32[64,2048]{1,0:T(8,128)}, f32[64,2048]{1,0:T(8,128)}, f32[64,2048]{1,0:T(8,128)}, f32[64,512]{1,0:T(8,128)}, /*index=5*/f32[64,512]{1,0:T(8,128)}, f32[64,512]{1,0:T(8,128)}) custom-call(bf16[64,8192]{1,0:T(8,128)(2,1)} %get-tuple-element.17.refs_0_, f32[64,2048]{1,0:T(8,128)} %get-tuple-element.18.refs_1_, ...), custom_call_target="tpu_custom_call" | custom-call | bytes 4194304 | tf_op jit(solution)/shard_map/adamw_tail/pallas_call | solution.py:344

commit v4 on v3

--- a/solution.py
+++ b/solution.py
@@ -45,7 +45,7 @@
     hidden_hbm, cot_hbm, frozen_hbm, down_hbm, up_hbm,
     hgrad_ref, gdown_ref, gup_ref,
     cot, mc, upf, dfac, frozen, hidv, hid,
-    lr_c, lr_y, part, crecv, ysend, yrecv,
+    lr_c, lr_y, part, csend, crecv, ysend, yrecv,
     up_placed, up_placed_t, down_placed_t,
     xsend, xrecv, gown, zsend, zrecv,
     load_sem, hs, hr, lcs, lcr, lys, lyr, cs, cr, ys, yr, xs, xr, zs, zr,
@@ -79,10 +79,10 @@
 
     cot_load = pltpu.make_async_copy(cot_hbm, cot, load_sem.at[0])
     upf_load = pltpu.make_async_copy(up_hbm, upf, load_sem.at[1])
+    hid_load = pltpu.make_async_copy(hidden_hbm, hidv, load_sem.at[3])
+    hid_load.start()
     cot_load.start()
     upf_load.start()
-    hid_load = pltpu.make_async_copy(hidden_hbm, hidv, load_sem.at[3])
-    hid_load.start()
     order = [lax.rem(2 * (y + 1) + i, T) for i in range(T)]
     frozen_loads = []
     for i, j in enumerate(order):
@@ -160,15 +160,6 @@
         for s in range(S):
             ref[s % 2, pl.ds((s // 2) * K, K), :] = turned[s * K:(s + 1) * K].astype(BF16)
 
-    cot_load.wait()
-    row = lax.broadcasted_iota(jnp.int32, (R, C), 0)
-    mc[...] = jnp.where(row < live_ref[p], cot[...].astype(F32), 0.0).astype(BF16)
-    upf_load.wait()
-    up_own = own_slot(dot_nt(mc[...], upf[...]))
-    pl.semaphore_wait(barrier, len(peers))
-    up_core = core_exchange(0, up_own)
-
-    hid_load.wait()
     hid_sends, hid_recvs = [], []
 
     def send_hidden(i):
@@ -185,10 +176,18 @@
         hid_recvs.append(recvs)
         hid[i, my_rows] = hidv[:, pl.ds(pl.multiple_of(m * Wc + i * Q, Q), Q)]
 
-    send_hidden(0)
-    up_recvs = y_exchange(0, up_core)
-    for i in range(1, NG):
+    hid_load.wait()
+    pl.semaphore_wait(barrier, len(peers))
+    early = NG // 2
+    for i in range(early - 1):
         send_hidden(i)
+
+    cot_load.wait()
+    row = lax.broadcasted_iota(jnp.int32, (R, C), 0)
+    mc[...] = jnp.where(row < live_ref[p], cot[...].astype(F32), 0.0).astype(BF16)
+    upf_load.wait()
+    up_own = own_slot(dot_nt(mc[...], upf[...]))
+    up_core = core_exchange(0, up_own)
 
     tile = min(512, Wc)
 
@@ -210,11 +209,18 @@
 
     def core_send(i):
         j = order[i]
-        cp = remote(part.at[j, oc], crecv.at[j], cs.at[i], cr.at[i], core_peer)
+        csend[j] = part[j, oc].astype(BF16)
+        cp = remote(csend.at[j], crecv.at[j], cs.at[i], cr.at[i], core_peer)
         cp.start()
         core_copies.append(cp)
 
-    for i in range(T - 2):
+    send_hidden(early - 1)
+    frozen_chunk(0)
+    core_send(0)
+    up_recvs = y_exchange(0, up_core)
+    for i in range(early, NG):
+        send_hidden(i)
+    for i in range(1, T - 2):
         frozen_chunk(i)
         core_send(i)
 
@@ -243,14 +249,14 @@
         core_copies[i].wait_recv()
         for k in range(1, Y):
             to = lax.rem(y + k, Y)
-            ysend[k - 1, j] = (part[j, c, to] + crecv[j, to]).astype(BF16)
+            ysend[k - 1, j] = (part[j, c, to] + crecv[j, to].astype(F32)).astype(BF16)
             cp = remote(
                 ysend.at[k - 1, j], yrecv.at[k - 1, j], ys.at[k - 1, j], yr.at[k - 1, j],
                 y_peers[k - 1],
             )
             cp.start()
             y_copies.append(cp)
-        part[j, c, y] = part[j, c, y] + crecv[j, y]
+        part[j, c, y] = part[j, c, y] + crecv[j, y].astype(F32)
 
     z_copies = []
 
@@ -267,6 +273,7 @@
             z_copies.append(cp)
 
     dfac_load.wait()
+    down_grad_chunk(0)
     for i in range(T - 2, T):
         frozen_chunk(i)
 
@@ -277,20 +284,26 @@
             part[m, q % 2, q // 2, :, cols] += res[q * r:(q + 1) * r]
         return carry
 
-    down_grad_chunk(0)
     lax.fori_loop(0, Wc // tile, extra_tile, 0)
     for i in range(T - 2, T):
         core_send(i)
+    down_grad_chunk(1)
     core_sum(0)
-    for i in range(1, NG):
+    for i in range(2, early):
+        down_grad_chunk(i)
+    core_sum(1)
+    for i in range(early, NG - 2):
+        down_grad_chunk(i)
+    pair_sum(0)
+    for i in range(NG - 2, NG):
         down_grad_chunk(i)
     down_part = dot_nn(hid[0], dfac[:Q, :])
     for i in range(1, NG):
         down_part = down_part + dot_nn(hid[i], dfac[i * Q:(i + 1) * Q, :])
     down_core = core_exchange(1, own_slot(down_part))
-    pair_sum(0)
+    pair_sum(1)
     down_recvs = y_exchange(1, down_core)
-    for i in range(1, T):
+    for i in range(2, T):
         core_sum(i)
         pair_sum(i)
     place_transposed(down_placed_t, gathered(1, down_recvs))
@@ -388,7 +401,7 @@
             V((R, C), BF16), V((R, C), BF16), V((D * K, C), BF16), V((Wc, D * K), BF16),
             V((W, C), BF16), V((r, W), BF16), V((NG, R, Q), BF16),
             V((2, 2, R // 2, 2 * K), F32), V((2, Y, R // 2, 2 * K), F32),
-            V((T, 2, Y, r, Wc), F32), V((T, Y, r, Wc), F32),
+            V((T, 2, Y, r, Wc), F32), V((T, Y, r, Wc), BF16), V((T, Y, r, Wc), BF16),
             V((Y - 1, T, r, Wc), BF16), V((Y - 1, T, r, Wc), BF16),
             V((R, D * K), BF16), V((2, A * K, R), BF16), V((2, A * K, R), BF16),
             V((NC, A, K, Q), BF16), V((NC, A, K, Q), BF16), V((NC, A, K, Q), F32),

time: 59.1 us -> 60.7 us (1.027)
  Pallas kernels: 58.2 us -> 59.8 us
    pallas_call x1, Pallas kernels: 53.8 us -> 55.4 us  [local(): pl.pallas_call(functools.partial(kernel, D, T, R, W, C), out_shape=(jax.S...]
where the time goes in v4:
time: 60.7 us; the launch traced here: 60.5 us
  Pallas kernels  59.8 us (99%)
  between operations  0.64 us (1%)
    pallas_call x1, Pallas kernels, local(): pl.pallas_call(functools.partial(kernel, D, T, R, W, C), out_shape=(jax.S...  55.4 us
    pallas_call x1, Pallas kernels, tail(): pl.pallas_call(tail_kernel, grid=(steps,), out_shape=(jax.ShapeDtypeStruc...  4.37 us

profile of v4, /device:TPU:0, one launch (start us, length us, event | category | flops | bytes accessed | tf_op | source)
XLA Modules:
  0.0 60.5 jit_solution(5257412445355034521)
XLA Ops:
  0.6 55.4 %lora_backward.1 = (bf16[64,8192]{1,0:T(8,128)(2,1)}, f32[64,2048]{1,0:T(8,128)}, f32[64,512]{1,0:T(8,128)}) custom-call(s32[1,256]{1,0:T(1,128)} %bitcast.10, s32[8]{0:T(128)} %bucket_ref.1, s32[8]{0:T(128)} %owner_ref.1, s32[8]{0:T(128)} %live_ref.1, bf16[64,8192]{1,0:T(8,128)(2,1)} %hidden_hbm.1, bf16[256,512]{1,0:T(8,128)(2,1)} %cot_hbm.1, ...), custom_call_target="tpu_custom_call" | custom-call | flops 2147483648 | bytes 8388608 | tf_op jit(solution)/shard_map/lora_backward/pallas_call | solution.py:391
  56.1 4.4 %adamw_tail.1 = (bf16[64,8192]{1,0:T(8,128)(2,1)}, f32[64,2048]{1,0:T(8,128)}, f32[64,2048]{1,0:T(8,128)}, f32[64,2048]{1,0:T(8,128)}, f32[64,512]{1,0:T(8,128)}, /*index=5*/f32[64,512]{1,0:T(8,128)}, f32[64,512]{1,0:T(8,128)}) custom-call(bf16[64,8192]{1,0:T(8,128)(2,1)} %get-tuple-element.17.refs_0_, f32[64,2048]{1,0:T(8,128)} %get-tuple-element.18.refs_1_, ...), custom_call_target="tpu_custom_call" | custom-call | bytes 4194304 | tf_op jit(solution)/shard_map/adamw_tail/pallas_call | solution.py:357

commit v5 on v4

--- a/solution.py
+++ b/solution.py
@@ -45,7 +45,7 @@
     hidden_hbm, cot_hbm, frozen_hbm, down_hbm, up_hbm,
     hgrad_ref, gdown_ref, gup_ref,
     cot, mc, upf, dfac, frozen, hidv, hid,
-    lr_c, lr_y, part, csend, crecv, ysend, yrecv,
+    lr_c, lr_y, part, crecv, ysend, yrecv,
     up_placed, up_placed_t, down_placed_t,
     xsend, xrecv, gown, zsend, zrecv,
     load_sem, hs, hr, lcs, lcr, lys, lyr, cs, cr, ys, yr, xs, xr, zs, zr,
@@ -56,7 +56,7 @@
     Y = T // 2
     r = R // T
     Wc = W // T
-    Q = C // 2
+    Q = C
     NG = Wc // Q
     NU = C // Q
     p = lax.axis_index("dp")
@@ -105,6 +105,10 @@
         hit = tok_col == i
         slot_of = jnp.where(hit, owner_ref[i], slot_of)
         bucket = jnp.where(hit, bucket_ref[i], bucket)
+    slot_row = jnp.zeros((1, R), jnp.int32)
+    for i in range(S):
+        slot_row = jnp.where(tok_ref[...] == i, owner_ref[i], slot_row)
+    slot_row = jnp.broadcast_to(slot_row, (K, R))
     steps_up = (
         1
         + (bucket >= 1).astype(jnp.int32)
@@ -152,13 +156,13 @@
         for i in range(1, Y):
             total = total + lr_y[kind, i]
         own = jnp.concatenate([total[:, :K], total[:, K:]], axis=0)
-        weight = (own * factor).astype(BF16).astype(F32)
-        return jnp.concatenate([jnp.where(slot_of == s, weight, 0.0) for s in range(S)], axis=1)
-
-    def place_transposed(ref, placed):
-        turned = placed.T
+        return (own * factor).astype(BF16).astype(F32)
+
+    def place_transposed(ref, weight):
+        turned = weight.T
         for s in range(S):
-            ref[s % 2, pl.ds((s // 2) * K, K), :] = turned[s * K:(s + 1) * K].astype(BF16)
+            rows = pl.ds(lax.rem(s % 2 + ob, 2) * (A * K) + (s // 2) * K, K)
+            ref[rows, :] = jnp.where(slot_row == s, turned, 0.0).astype(BF16)
 
     hid_sends, hid_recvs = [], []
 
@@ -178,9 +182,7 @@
 
     hid_load.wait()
     pl.semaphore_wait(barrier, len(peers))
-    early = NG // 2
-    for i in range(early - 1):
-        send_hidden(i)
+    send_hidden(0)
 
     cot_load.wait()
     row = lax.broadcasted_iota(jnp.int32, (R, C), 0)
@@ -209,33 +211,32 @@
 
     def core_send(i):
         j = order[i]
-        csend[j] = part[j, oc].astype(BF16)
-        cp = remote(csend.at[j], crecv.at[j], cs.at[i], cr.at[i], core_peer)
+        cp = remote(part.at[j, oc], crecv.at[j], cs.at[i], cr.at[i], core_peer)
         cp.start()
         core_copies.append(cp)
 
-    send_hidden(early - 1)
+    send_hidden(1)
     frozen_chunk(0)
     core_send(0)
     up_recvs = y_exchange(0, up_core)
-    for i in range(early, NG):
+    for i in range(2, NG):
         send_hidden(i)
     for i in range(1, T - 2):
         frozen_chunk(i)
         core_send(i)
 
-    placed = gathered(0, up_recvs)
-    up_placed[...] = placed.astype(BF16)
-    place_transposed(up_placed_t, placed)
+    up_weight = gathered(0, up_recvs)
+    place_transposed(up_placed_t, up_weight)
 
     x_copies = []
 
     def grad_chunk(i, left, right):
-        xsend[i] = dot_nn(left[ob], right).astype(BF16).reshape(A, K, Q)
+        both = dot_nn(left[...], right)
+        xsend[i] = both[: A * K].astype(BF16).reshape(A, K, Q)
         cp = remote(xsend.at[i], xrecv.at[i], xs.at[i], xr.at[i], x_peer)
         cp.start()
         x_copies.append(cp)
-        gown[i] = dot_nn(left[b], right).reshape(A, K, Q)
+        gown[i] = both[A * K:].reshape(A, K, Q)
 
     def down_grad_chunk(i):
         for rcv in hid_recvs[i]:
@@ -249,14 +250,14 @@
         core_copies[i].wait_recv()
         for k in range(1, Y):
             to = lax.rem(y + k, Y)
-            ysend[k - 1, j] = (part[j, c, to] + crecv[j, to].astype(F32)).astype(BF16)
+            ysend[k - 1, j] = (part[j, c, to] + crecv[j, to]).astype(BF16)
             cp = remote(
                 ysend.at[k - 1, j], yrecv.at[k - 1, j], ys.at[k - 1, j], yr.at[k - 1, j],
                 y_peers[k - 1],
             )
             cp.start()
             y_copies.append(cp)
-        part[j, c, y] = part[j, c, y] + crecv[j, y].astype(F32)
+        part[j, c, y] = part[j, c, y] + crecv[j, y]
 
     z_copies = []
 
@@ -277,6 +278,10 @@
     for i in range(T - 2, T):
         frozen_chunk(i)
 
+    up_placed[...] = jnp.concatenate(
+        [jnp.where(slot_of == s, up_weight, 0.0) for s in range(S)], axis=1
+    ).astype(BF16)
+
     def extra_tile(t, carry):
         cols = pl.ds(pl.multiple_of(t * tile, tile), tile)
         res = dot_nt(up_placed[...], dfac[cols, :])
@@ -289,27 +294,23 @@
         core_send(i)
     down_grad_chunk(1)
     core_sum(0)
-    for i in range(2, early):
-        down_grad_chunk(i)
+    down_grad_chunk(2)
     core_sum(1)
-    for i in range(early, NG - 2):
-        down_grad_chunk(i)
+    down_grad_chunk(3)
     pair_sum(0)
-    for i in range(NG - 2, NG):
-        down_grad_chunk(i)
     down_part = dot_nn(hid[0], dfac[:Q, :])
     for i in range(1, NG):
         down_part = down_part + dot_nn(hid[i], dfac[i * Q:(i + 1) * Q, :])
     down_core = core_exchange(1, own_slot(down_part))
+    core_sum(2)
     pair_sum(1)
     down_recvs = y_exchange(1, down_core)
-    for i in range(2, T):
+    for i in range(3, T):
         core_sum(i)
-        pair_sum(i)
     place_transposed(down_placed_t, gathered(1, down_recvs))
     for i in range(NU):
         grad_chunk(NG + i, down_placed_t, mc[:, i * Q:(i + 1) * Q])
-    for i in range(T, NG + NU):
+    for i in range(2, NG + NU):
         pair_sum(i)
 
     def last_grad(i):
@@ -380,7 +381,7 @@
     W = hidden.shape[1]
     K = PADDED_RANK
     A, Y, r, Wc = D // 2, T // 2, R // T, W // T
-    Q = C // 2
+    Q = C
     NG = Wc // Q
     NC = NG + C // Q
     vmem = pl.BlockSpec(memory_space=pltpu.VMEM)
@@ -401,9 +402,9 @@
             V((R, C), BF16), V((R, C), BF16), V((D * K, C), BF16), V((Wc, D * K), BF16),
             V((W, C), BF16), V((r, W), BF16), V((NG, R, Q), BF16),
             V((2, 2, R // 2, 2 * K), F32), V((2, Y, R // 2, 2 * K), F32),
-            V((T, 2, Y, r, Wc), F32), V((T, Y, r, Wc), BF16), V((T, Y, r, Wc), BF16),
+            V((T, 2, Y, r, Wc), F32), V((T, Y, r, Wc), F32),
             V((Y - 1, T, r, Wc), BF16), V((Y - 1, T, r, Wc), BF16),
-            V((R, D * K), BF16), V((2, A * K, R), BF16), V((2, A * K, R), BF16),
+            V((R, D * K), BF16), V((D * K, R), BF16), V((D * K, R), BF16),
             V((NC, A, K, Q), BF16), V((NC, A, K, Q), BF16), V((NC, A, K, Q), F32),
             V((A - 1, NC, K, Q), BF16), V((A - 1, NC, K, Q), BF16),
             dma((4 + T,)), dma((T - 1, NG)), dma((T - 1, NG)),

time: 60.7 us -> 63.3 us (1.043)
  Pallas kernels: 59.8 us -> 62.4 us
    pallas_call x1, Pallas kernels: 55.4 us -> 58 us  [local(): pl.pallas_call(functools.partial(kernel, D, T, R, W, C), out_shape=(jax.S...]
where the time goes in v5:
time: 63.3 us; the launch traced here: 63.1 us
  Pallas kernels  62.4 us (99%)
  between operations  0.64 us (1%)
    pallas_call x1, Pallas kernels, local(): pl.pallas_call(functools.partial(kernel, D, T, R, W, C), out_shape=(jax.S...  58 us
    pallas_call x1, Pallas kernels, tail(): pl.pallas_call(tail_kernel, grid=(steps,), out_shape=(jax.ShapeDtypeStruc...  4.37 us

profile of v5, /device:TPU:0, one launch (start us, length us, event | category | flops | bytes accessed | tf_op | source)
XLA Modules:
  0.0 63.1 jit_solution(10878193298132871729)
XLA Ops:
  0.6 58.0 %lora_backward.1 = (bf16[64,8192]{1,0:T(8,128)(2,1)}, f32[64,2048]{1,0:T(8,128)}, f32[64,512]{1,0:T(8,128)}) custom-call(s32[1,256]{1,0:T(1,128)} %bitcast.10, s32[8]{0:T(128)} %bucket_ref.1, s32[8]{0:T(128)} %owner_ref.1, s32[8]{0:T(128)} %live_ref.1, bf16[64,8192]{1,0:T(8,128)(2,1)} %hidden_hbm.1, bf16[256,512]{1,0:T(8,128)(2,1)} %cot_hbm.1, ...), custom_call_target="tpu_custom_call" | custom-call | flops 2147483648 | bytes 8388608 | tf_op jit(solution)/shard_map/lora_backward/pallas_call | solution.py:392
  58.7 4.4 %adamw_tail.1 = (bf16[64,8192]{1,0:T(8,128)(2,1)}, f32[64,2048]{1,0:T(8,128)}, f32[64,2048]{1,0:T(8,128)}, f32[64,2048]{1,0:T(8,128)}, f32[64,512]{1,0:T(8,128)}, /*index=5*/f32[64,512]{1,0:T(8,128)}, f32[64,512]{1,0:T(8,128)}) custom-call(bf16[64,8192]{1,0:T(8,128)(2,1)} %get-tuple-element.17.refs_0_, f32[64,2048]{1,0:T(8,128)} %get-tuple-element.18.refs_1_, ...), custom_call_target="tpu_custom_call" | custom-call | bytes 4194304 | tf_op jit(solution)/shard_map/adamw_tail/pallas_call | solution.py:358

commit v6 on v5

--- a/solution.py
+++ b/solution.py
@@ -56,7 +56,7 @@
     Y = T // 2
     r = R // T
     Wc = W // T
-    Q = C
+    Q = C // 2
     NG = Wc // Q
     NU = C // Q
     p = lax.axis_index("dp")
@@ -180,16 +180,18 @@
         hid_recvs.append(recvs)
         hid[i, my_rows] = hidv[:, pl.ds(pl.multiple_of(m * Wc + i * Q, Q), Q)]
 
-    hid_load.wait()
-    pl.semaphore_wait(barrier, len(peers))
-    send_hidden(0)
-
     cot_load.wait()
     row = lax.broadcasted_iota(jnp.int32, (R, C), 0)
     mc[...] = jnp.where(row < live_ref[p], cot[...].astype(F32), 0.0).astype(BF16)
     upf_load.wait()
     up_own = own_slot(dot_nt(mc[...], upf[...]))
+    pl.semaphore_wait(barrier, len(peers))
     up_core = core_exchange(0, up_own)
+    hid_load.wait()
+    send_hidden(0)
+    up_recvs = y_exchange(0, up_core)
+    for i in range(1, NG):
+        send_hidden(i)
 
     tile = min(512, Wc)
 
@@ -215,15 +217,8 @@
         cp.start()
         core_copies.append(cp)
 
-    send_hidden(1)
     frozen_chunk(0)
     core_send(0)
-    up_recvs = y_exchange(0, up_core)
-    for i in range(2, NG):
-        send_hidden(i)
-    for i in range(1, T - 2):
-        frozen_chunk(i)
-        core_send(i)
 
     up_weight = gathered(0, up_recvs)
     place_transposed(up_placed_t, up_weight)
@@ -273,11 +268,14 @@
             cp.start()
             z_copies.append(cp)
 
+    down_grad_chunk(0)
+    for i in range(1, T):
+        frozen_chunk(i)
+        if i < T - 2:
+            core_send(i)
+        if i < 3:
+            down_grad_chunk(i)
     dfac_load.wait()
-    down_grad_chunk(0)
-    for i in range(T - 2, T):
-        frozen_chunk(i)
-
     up_placed[...] = jnp.concatenate(
         [jnp.where(slot_of == s, up_weight, 0.0) for s in range(S)], axis=1
     ).astype(BF16)
@@ -292,25 +290,29 @@
     lax.fori_loop(0, Wc // tile, extra_tile, 0)
     for i in range(T - 2, T):
         core_send(i)
-    down_grad_chunk(1)
+    down_grad_chunk(3)
     core_sum(0)
-    down_grad_chunk(2)
+    pair_sum(0)
+    down_grad_chunk(4)
+    down_grad_chunk(5)
+    pair_sum(1)
     core_sum(1)
-    down_grad_chunk(3)
-    pair_sum(0)
+    down_grad_chunk(6)
+    down_grad_chunk(7)
     down_part = dot_nn(hid[0], dfac[:Q, :])
     for i in range(1, NG):
         down_part = down_part + dot_nn(hid[i], dfac[i * Q:(i + 1) * Q, :])
     down_core = core_exchange(1, own_slot(down_part))
-    core_sum(2)
-    pair_sum(1)
+    pair_sum(2)
     down_recvs = y_exchange(1, down_core)
-    for i in range(3, T):
+    for i in range(2, T):
         core_sum(i)
+        if i + 1 < NG:
+            pair_sum(i + 1)
     place_transposed(down_placed_t, gathered(1, down_recvs))
     for i in range(NU):
         grad_chunk(NG + i, down_placed_t, mc[:, i * Q:(i + 1) * Q])
-    for i in range(2, NG + NU):
+    for i in range(min(T + 1, NG), NG + NU):
         pair_sum(i)
 
     def last_grad(i):
@@ -381,7 +383,7 @@
     W = hidden.shape[1]
     K = PADDED_RANK
     A, Y, r, Wc = D // 2, T // 2, R // T, W // T
-    Q = C
+    Q = C // 2
     NG = Wc // Q
     NC = NG + C // Q
     vmem = pl.BlockSpec(memory_space=pltpu.VMEM)

time: 63.3 us -> 57.6 us (0.910)
  Pallas kernels: 62.4 us -> 56.7 us
    pallas_call x1, Pallas kernels: 58 us -> 52.4 us  [local(): pl.pallas_call(functools.partial(kernel, D, T, R, W, C), out_shape=(jax.S...]
where the time goes in v6:
time: 57.6 us; the launch traced here: 57.4 us
  Pallas kernels  56.7 us (98%)
  between operations  0.64 us (1%)
    pallas_call x1, Pallas kernels, local(): pl.pallas_call(functools.partial(kernel, D, T, R, W, C), out_shape=(jax.S...  52.4 us
    pallas_call x1, Pallas kernels, tail(): pl.pallas_call(tail_kernel, grid=(steps,), out_shape=(jax.ShapeDtypeStruc...  4.37 us

profile of v6, /device:TPU:0, one launch (start us, length us, event | category | flops | bytes accessed | tf_op | source)
XLA Modules:
  0.0 57.4 jit_solution(18421485981052911288)
XLA Ops:
  0.6 52.4 %lora_backward.1 = (bf16[64,8192]{1,0:T(8,128)(2,1)}, f32[64,2048]{1,0:T(8,128)}, f32[64,512]{1,0:T(8,128)}) custom-call(s32[1,256]{1,0:T(1,128)} %bitcast.10, s32[8]{0:T(128)} %bucket_ref.1, s32[8]{0:T(128)} %owner_ref.1, s32[8]{0:T(128)} %live_ref.1, bf16[64,8192]{1,0:T(8,128)(2,1)} %hidden_hbm.1, bf16[256,512]{1,0:T(8,128)(2,1)} %cot_hbm.1, ...), custom_call_target="tpu_custom_call" | custom-call | flops 2147483648 | bytes 8388608 | tf_op jit(solution)/shard_map/lora_backward/pallas_call | solution.py:394
  53.0 4.4 %adamw_tail.1 = (bf16[64,8192]{1,0:T(8,128)(2,1)}, f32[64,2048]{1,0:T(8,128)}, f32[64,2048]{1,0:T(8,128)}, f32[64,2048]{1,0:T(8,128)}, f32[64,512]{1,0:T(8,128)}, /*index=5*/f32[64,512]{1,0:T(8,128)}, f32[64,512]{1,0:T(8,128)}) custom-call(bf16[64,8192]{1,0:T(8,128)(2,1)} %get-tuple-element.17.refs_0_, f32[64,2048]{1,0:T(8,128)} %get-tuple-element.18.refs_1_, ...), custom_call_target="tpu_custom_call" | custom-call | bytes 4194304 | tf_op jit(solution)/shard_map/adamw_tail/pallas_call | solution.py:360
